TPU v7x, 256 devices: a whole 4x4x8 slice. The times are simulated.
256 devices in a mesh: section: 16 (over y, x_hi, core), fsdp: 16 (over z, x_lo).
Axes of the slice: x: 4 (x_hi: 2, x_lo: 2; x = x_hi * 2 + x_lo), y: 4, z: 8, core: 2. Of those that a mesh axis runs over, the one named last changes fastest.
Arguments:
- embeddings: bfloat16 [4, 1024, 2048], P(None, 'fsdp'), may hold values from -6 to 6
- section_weights: bfloat16 [16, 2048, 2048], P('section', 'fsdp'), may hold values from -0.125 to 0.125
- section_gains: bfloat16 [16, 2048], P('section', 'fsdp'), may hold values from 0.099609375 to 1.8984375
- top_direction: bfloat16 [4, 1024, 2048], P(None, 'fsdp'), may hold values from -6 to 6
- new_logprob: float32 [4, 1024], P(None, 'fsdp'), may hold values from -3 to -0.1
- old_logprob: float32 [4, 1024], P(None, 'fsdp'), may hold values from -3 to -0.1
- segment_ids: int32 [4, 1024], P(None, 'fsdp'), may hold values from 0 to 3, never falling along the last dimension, each value on 1 to 512 neighbouring positions
- advantages: float32 [4, 4], replicated, may hold values from -4 to 4
Outputs:
- weight_grad: float32 [16, 2048, 2048], P('section', 'fsdp')
- gain_grad: float32 [16, 2048], P('section', 'fsdp')
- gspo_loss: float32 [], replicated
Inputs may be any that keep to these rules, and one draw needn't show every extreme that they name: `segment_ids`: in each micro-batch the numbers never fall along the tokens, every sequence 0 to 3 has 1 to 512 tokens, and one has exactly 512.
All inputs are finite; a program needn't handle non-finite values.
Results may differ from a plain program's by a relative error of at most 0.035.
Values may be sent and summed in bfloat16 or wider, within the bound.
No kernel may reach another device: no remote copies, remote signals or barrier semaphores. Data moves between devices by JAX's collectives and lax.ppermute only.
A program may use at most 64 MiB of HBM per device.

v0:
```python
import jax
import jax.numpy as jnp
from jax import lax
from jax.sharding import PartitionSpec as P

clip_epsilon = 0.2
norm_epsilon = 1e-05


def passed_along(block, axis, distance):
    devices = range(lax.axis_size(axis))
    route = [(i - distance, i) for i in devices if i - distance in devices]
    return lax.ppermute(block, axis, route)


def layer_forward(states, matrix, gain_vec):
    widened = states.astype(jnp.float32)
    inverse_rms = lax.rsqrt(jnp.mean(widened * widened, axis=-1, keepdims=True) + norm_epsilon)
    normed = (widened * inverse_rms * gain_vec).astype(jnp.bfloat16)
    projected = jnp.dot(normed, matrix, preferred_element_type=jnp.float32)
    output = (widened + jax.nn.silu(projected)).astype(jnp.bfloat16)
    return (normed, projected, inverse_rms, output)


def layer_backward(upstream, states, projected, inverse_rms, matrix, gain_vec):
    sigmoid_pre = jax.nn.sigmoid(projected)
    upstream_f = upstream.astype(jnp.float32)
    pre_grad = (upstream_f * sigmoid_pre * (1.0 + projected * (1.0 - sigmoid_pre))).astype(
        jnp.bfloat16
    )
    norm_grad = lax.dot_general(
        pre_grad, matrix, (((1,), (1,)), ((), ())), preferred_element_type=jnp.float32
    )
    widened = states.astype(jnp.float32)
    scaled_grad = gain_vec * norm_grad
    input_grad = inverse_rms * scaled_grad - widened * inverse_rms**3 * jnp.mean(
        scaled_grad * widened, axis=-1, keepdims=True
    )
    passed = (upstream_f + input_grad).astype(jnp.bfloat16)
    gain_grad = jnp.sum(norm_grad * widened * inverse_rms, axis=0)
    return (pre_grad, passed, gain_grad)


def store_slot(buffer, value, position, enabled):
    previous = lax.dynamic_index_in_dim(buffer, position, 0, keepdims=False)
    chosen = jnp.where(enabled, value, previous)
    return lax.dynamic_update_index_in_dim(buffer, chosen, position, 0)


def local(
    embeddings,
    section_weights,
    section_gains,
    top_direction,
    new_logprob,
    old_logprob,
    segment_ids,
    advantages,
):
    sections = lax.axis_size("section")
    section_index = lax.axis_index("section")
    micro_batches, row_count, feature_count = embeddings.shape
    seq_count = advantages.shape[1]
    labels = lax.broadcasted_iota(jnp.int32, (1, 1, seq_count), 2)
    member = (segment_ids[:, :, None] == labels).astype(jnp.float32)
    log_drift = new_logprob - old_logprob
    part_sums = jnp.sum(log_drift[:, :, None] * member, axis=1)
    part_counts = jnp.sum(member, axis=1)
    seq_sums, seq_counts = lax.psum((part_sums, part_counts), "fsdp")
    seq_ratio = jnp.exp(seq_sums / seq_counts)
    clipped = jnp.clip(seq_ratio, 1.0 - clip_epsilon, 1.0 + clip_epsilon)
    plain_term = seq_ratio * advantages
    bounded_term = clipped * advantages
    gspo_loss = -jnp.sum(jnp.minimum(plain_term, bounded_term))
    per_seq = jnp.where(plain_term <= bounded_term, -advantages * seq_ratio / seq_counts, 0.0)
    token_coef = jnp.sum(member * per_seq[:, None, :], axis=2)
    gathered_w, gathered_g = (
        lax.all_gather(section_weights, "fsdp", axis=1, tiled=True),
        lax.all_gather(section_gains, "fsdp", axis=1, tiled=True),
    )
    layer_matrix = gathered_w[0]
    layer_gain = gathered_g[0].astype(jnp.float32)
    tick_count = micro_batches + sections - 1
    zero_states = jnp.zeros((row_count, feature_count), jnp.bfloat16)
    zero_wide = jnp.zeros((row_count, feature_count), jnp.float32)
    zero_scale = jnp.zeros((row_count, 1), jnp.float32)

    def run_forward(feed_rows):
        return layer_forward(feed_rows, layer_matrix, layer_gain)

    def no_forward(feed_rows):
        return (zero_states, zero_wide, zero_scale, zero_states)

    def forward_tick(step_index, state_tuple):
        incoming, saved_in, saved_norm, saved_proj, saved_scale = state_tuple
        slot_raw = step_index - section_index
        is_live = (slot_raw >= 0) & (slot_raw < micro_batches)
        slot_index = jnp.clip(slot_raw, 0, micro_batches - 1)
        fresh_rows = lax.dynamic_index_in_dim(embeddings, slot_index, 0, keepdims=False)
        feed_rows = jnp.where(section_index == 0, fresh_rows, incoming)
        normed, projected, inverse_rms, output = lax.cond(
            is_live, run_forward, no_forward, feed_rows
        )
        saved_in = store_slot(saved_in, feed_rows, slot_index, is_live)
        saved_norm = store_slot(saved_norm, normed, slot_index, is_live)
        saved_proj = store_slot(saved_proj, projected, slot_index, is_live)
        saved_scale = store_slot(saved_scale, inverse_rms, slot_index, is_live)
        incoming = passed_along(output, "section", 1)
        return (incoming, saved_in, saved_norm, saved_proj, saved_scale)

    start_forward = (
        zero_states,
        jnp.zeros((micro_batches, row_count, feature_count), jnp.bfloat16),
        jnp.zeros((micro_batches, row_count, feature_count), jnp.bfloat16),
        jnp.zeros((micro_batches, row_count, feature_count), jnp.float32),
        jnp.zeros((micro_batches, row_count, 1), jnp.float32),
    )
    done_forward = lax.fori_loop(0, tick_count, forward_tick, start_forward)
    saved_in, saved_norm, saved_proj, saved_scale = (
        done_forward[1],
        done_forward[2],
        done_forward[3],
        done_forward[4],
    )
    again_w, again_g = (
        lax.all_gather(section_weights, "fsdp", axis=1, tiled=True),
        lax.all_gather(section_gains, "fsdp", axis=1, tiled=True),
    )
    back_matrix = again_w[0]
    back_gain = again_g[0].astype(jnp.float32)
    zero_gain = jnp.zeros((feature_count,), jnp.float32)

    def backward_tick(step_index, state_tuple):
        incoming, saved_grad, gain_total = state_tuple
        slot_raw = step_index - (sections - 1 - section_index)
        is_live = (slot_raw >= 0) & (slot_raw < micro_batches)
        slot_index = jnp.clip(slot_raw, 0, micro_batches - 1)
        coef_rows = lax.dynamic_index_in_dim(token_coef, slot_index, 0, keepdims=False)
        direction_rows = lax.dynamic_index_in_dim(top_direction, slot_index, 0, keepdims=False)
        top_grad = (coef_rows[:, None] * direction_rows.astype(jnp.float32)).astype(jnp.bfloat16)
        upstream = jnp.where(section_index == sections - 1, top_grad, incoming)
        layer_in = lax.dynamic_index_in_dim(saved_in, slot_index, 0, keepdims=False)
        projected = lax.dynamic_index_in_dim(saved_proj, slot_index, 0, keepdims=False)
        inverse_rms = lax.dynamic_index_in_dim(saved_scale, slot_index, 0, keepdims=False)

        def run_backward(operands):
            return layer_backward(
                operands[0], operands[1], operands[2], operands[3], back_matrix, back_gain
            )

        def no_backward(operands):
            return (zero_states, zero_states, zero_gain)

        pre_grad, passed, gain_grad = lax.cond(
            is_live, run_backward, no_backward, (upstream, layer_in, projected, inverse_rms)
        )
        saved_grad = store_slot(saved_grad, pre_grad, slot_index, is_live)
        gain_total = gain_total + gain_grad
        incoming = passed_along(passed, "section", -1)
        return (incoming, saved_grad, gain_total)

    start_backward = (
        zero_states,
        jnp.zeros((micro_batches, row_count, feature_count), jnp.bfloat16),
        zero_gain,
    )
    done_backward = lax.fori_loop(0, tick_count, backward_tick, start_backward)
    saved_grad, gain_total = (done_backward[1], done_backward[2])
    flat_norm = saved_norm.reshape(micro_batches * row_count, feature_count)
    flat_grad = saved_grad.reshape(micro_batches * row_count, feature_count)
    weight_total = lax.dot_general(
        flat_norm, flat_grad, (((0,), (0,)), ((), ())), preferred_element_type=jnp.float32
    )
    weight_share, gain_share = (
        lax.psum_scatter(
            weight_total.astype(jnp.bfloat16), "fsdp", scatter_dimension=0, tiled=True
        ).astype(jnp.float32),
        lax.psum_scatter(
            gain_total.astype(jnp.bfloat16), "fsdp", scatter_dimension=0, tiled=True
        ).astype(jnp.float32),
    )
    return (weight_share[None], gain_share[None], gspo_loss)


def solution(mesh):
    placed = (
        P(None, "fsdp", None),
        P("section", "fsdp", None),
        P("section", "fsdp"),
        P(None, "fsdp", None),
        P(None, "fsdp"),
        P(None, "fsdp"),
        P(None, "fsdp"),
        P(),
    )
    return jax.shard_map(
        local,
        mesh=mesh,
        in_specs=placed,
        out_specs=(P("section", "fsdp", None), P("section", "fsdp"), P()),
        check_vma=False,
    )
```

profile of v0, /device:TPU:1, one launch (start us, length us, event | category | flops | bytes accessed | tf_op | source)
XLA Modules:
  0.0 981.1 jit_solution(17281906890773359639)
XLA Ops:
  8.0 33.0 %all_gather.8 = bf16[1,2048]{1,0:T(2,128)(2,1)S(1)} all-gather(bf16[1,128]{1,0:T(2,128)(2,1)} %param.18), channel_id=1, replica_groups=mesh['section'=16,'fsdp'=16] {'fsdp'}, dimensions={1}, use_global_device_ids=true | all-gather | bytes 4352 | tf_op jit(solution)/shard_map/all_gather | solution.py:79
  42.4 27.4 %all-reduce.1 = (f32[4,4]{1,0:T(4,128)S(1)}, f32[4,4]{1,0:T(4,128)S(1)}) all-reduce(f32[4,4]{1,0:T(4,128)S(1)} %get-tuple-element.653, f32[4,4]{1,0:T(4,128)S(1)} %get-tuple-element.652), channel_id=1, replica_groups=mesh['section'=16,'fsdp'=16] {'fsdp'}, use_global_device_ids=true, to_apply=%region_8.9 | all-reduce | flops 32 | bytes 256 | tf_op jit(solution)/shard_map/psum | solution.py:69
  71.9 125.6 %all-gather.2.cloned.1.call-done = bf16[1,2048,2048]{2,1,0:T(8,128)(2,1)} async-done(((bf16[1,128,2048]{2,1,0:T(8,128)(2,1)}), bf16[1,2048,2048]{2,1,0:T(8,128)(2,1)}) %all-gather.2.cloned.1.call-update) | async-done | bytes 8388624 | tf_op jit(solution)/shard_map/all_gather | solution.py:78
  199.9 271.3 %while.42 = (s32[]{:T(128)}, bf16[64,2048]{1,0:T(8,128)(2,1)S(1)}, bf16[4,64,2048]{2,1,0:T(8,128)(2,1)}, bf16[4,64,2048]{2,1,0:T(8,128)(2,1)}, f32[4,64,2048]{2,...) while((s32[]{:T(128)}, bf16[64,2048]{1,0:T(8,128)(2,1)S(1)}, ...), condition=%wide.region_4.5_spmd, body=%wide.region_0.4_spmd.sunk | while | flops 539230336 | bytes 17313868 | solution.py:118
  214.6 6.1 conditional.5
  228.7 6.1 conditional.5
  234.8 5.9 collective-permute-start
  246.8 6.1 conditional.5
  252.9 5.9 collective-permute-start
  264.8 6.1 conditional.5
  271.0 5.9 collective-permute-start
  283.7 11.2 %collective-permute-start = (bf16[64,2048]{1,0:T(8,128)(2,1)S(1)}, bf16[64,2048]{1,0:T(8,128)(2,1)S(1)}, u32[]{:S(2)}, u32[]{:S(2)}) collective-permute-start(bf16[64,2048]{1,0:T(8,128)(2,1)S(1)} %get-tuple-element.858), channel_id=1, source_target_pairs={{0,16},{16,32},{32,48},{48,64},{64,80},{80,96},{96,112},{112,128},... | collective-permute-start | bytes 786440 | tf_op jit(solution)/shard_map/while/body/eval_jaxpr/ppermute | solution.py:13
  301.8 5.9 collective-permute-start
  314.5 5.9 collective-permute-start
  352.8 6.0 collective-permute-start
  365.6 6.8 collective-permute-start
  379.2 6.8 collective-permute-start
  392.9 6.8 collective-permute-start
  406.5 6.8 collective-permute-start
  420.2 6.8 collective-permute-start
  433.8 6.8 collective-permute-start
  447.5 6.8 collective-permute-start
  461.1 6.8 collective-permute-start
  472.4 310.7 %while.43 = (s32[]{:T(128)}, bf16[64,2048]{1,0:T(8,128)(2,1)S(1)}, bf16[4,64,2048]{2,1,0:T(8,128)(2,1)}, f32[2048]{0:T(1024)S(1)}, s32[]{:T(128)}, /*index=5*/f3...) while((s32[]{:T(128)}, bf16[64,2048]{1,0:T(8,128)(2,1)S(1)}, ...), condition=%wide.region_15.16_spmd.clone, body=%wide.region_10.15_spmd.clone.sunk | while | flops 541067392 | bytes 15257740 | solution.py:167
  478.0 7.1 collective-permute-done.1
  501.8 7.1 collective-permute-done.1
  514.4 6.4 collective-permute-done.1
  526.4 6.4 collective-permute-done.1
  538.4 6.4 collective-permute-done.1
  550.3 6.4 collective-permute-done.1
  562.3 6.4 collective-permute-done.1
  574.2 6.4 collective-permute-done.1
  586.2 6.4 collective-permute-done.1
  598.2 6.4 collective-permute-done.1
  610.1 6.4 collective-permute-done.1
  622.1 6.4 collective-permute-done.1
  634.0 60.5 %collective-permute-done.1 = bf16[64,2048]{1,0:T(8,128)(2,1)S(1)} collective-permute-done((bf16[64,2048]{1,0:T(8,128)(2,1)S(1)}, bf16[64,2048]{1,0:T(8,128)(2,1)S(1)}, u32[]{:S(2)}, u32[]{:S(2)}) %collective-permute-start.1) | collective-permute-done | bytes 262176 | tf_op jit(solution)/shard_map/while/body/eval_jaxpr/ppermute | solution.py:13
  695.6 8.4 conditional.6
  696.6 6.2 fusion.14
  715.2 8.4 conditional.6
  716.2 6.2 fusion.14
  734.9 8.4 conditional.6
  735.8 6.2 fusion.14
  754.5 8.4 conditional.6
  755.4 6.2 fusion.14
  783.1 7.1 bitcast_convert_fusion
  792.2 34.5 %all-reduce = bf16[2048]{0:T(1024)(128)(2,1)S(1)} all-reduce(bf16[2048]{0:T(1024)(128)(2,1)S(1)} %convert_element_type.92), channel_id=3, replica_groups=mesh['section'=16,'fsdp'=16] {'fsdp'}, use_global_device_ids=true, to_apply=%region_17.18.clone | all-reduce | flops 2048 | bytes 8192
  827.3 143.7 %reduce-scatter.2.cloned.1.call-done = bf16[128,2048]{1,0:T(8,128)(2,1)} async-done(((bf16[2048,2048]{1,0:T(8,128)(2,1)}), bf16[128,2048]{1,0:T(8,128)(2,1)}) %reduce-scatter.2.cloned.1.call-update) | async-done | bytes 524304 | tf_op jit(solution)/shard_map/reduce_scatter | solution.py:175
  (485 shorter events, 350.5 us)
Async XLA Ops:
  7.2 190.3 %all-gather.2.cloned.1.call-start = ((), (), s32[]{:S(2)}) async-start(), calls=%async_computation.1 | async-start | bytes 8912896 | tf_op jit(solution)/shard_map/all_gather | solution.py:78
  7.9 963.1 %reduce-scatter.2.cloned.1.call-start = ((), (), s32[]{:S(2)}) async-start(), calls=%async_computation.2 | async-start | bytes 8912896 | tf_op jit(solution)/shard_map/reduce_scatter | solution.py:175
  203.5 8.3 collective-permute-start
  220.7 5.2 collective-permute-start
  234.8 9.2 collective-permute-start
  252.9 9.2 collective-permute-start
  271.0 9.2 collective-permute-start
  283.7 14.5 %collective-permute-start = (bf16[64,2048]{1,0:T(8,128)(2,1)S(1)}, bf16[64,2048]{1,0:T(8,128)(2,1)S(1)}, u32[]{:S(2)}, u32[]{:S(2)}) collective-permute-start(bf16[64,2048]{1,0:T(8,128)(2,1)S(1)} %get-tuple-element.858), channel_id=1, source_target_pairs={{0,16},{16,32},{32,48},{48,64},{64,80},{80,96},{96,112},{112,128},... | collective-permute-start | bytes 786440 | tf_op jit(solution)/shard_map/while/body/eval_jaxpr/ppermute | solution.py:13
  301.8 9.2 collective-permute-start
  314.5 9.2 collective-permute-start
  327.3 9.2 collective-permute-start
  340.0 9.2 collective-permute-start
  352.8 9.3 collective-permute-start
  365.6 10.1 %collective-permute-start = (bf16[64,2048]{1,0:T(8,128)(2,1)S(1)}, bf16[64,2048]{1,0:T(8,128)(2,1)S(1)}, u32[]{:S(2)}, u32[]{:S(2)}) collective-permute-start(bf16[64,2048]{1,0:T(8,128)(2,1)S(1)} %get-tuple-element.858), channel_id=1, source_target_pairs={{0,16},{16,32},{32,48},{48,64},{64,80},{80,96},{96,112},{112,128},... | collective-permute-start | bytes 786440 | tf_op jit(solution)/shard_map/while/body/eval_jaxpr/ppermute | solution.py:13
  379.2 10.1 %collective-permute-start = (bf16[64,2048]{1,0:T(8,128)(2,1)S(1)}, bf16[64,2048]{1,0:T(8,128)(2,1)S(1)}, u32[]{:S(2)}, u32[]{:S(2)}) collective-permute-start(bf16[64,2048]{1,0:T(8,128)(2,1)S(1)} %get-tuple-element.858), channel_id=1, source_target_pairs={{0,16},{16,32},{32,48},{48,64},{64,80},{80,96},{96,112},{112,128},... | collective-permute-start | bytes 786440 | tf_op jit(solution)/shard_map/while/body/eval_jaxpr/ppermute | solution.py:13
  392.9 10.1 %collective-permute-start = (bf16[64,2048]{1,0:T(8,128)(2,1)S(1)}, bf16[64,2048]{1,0:T(8,128)(2,1)S(1)}, u32[]{:S(2)}, u32[]{:S(2)}) collective-permute-start(bf16[64,2048]{1,0:T(8,128)(2,1)S(1)} %get-tuple-element.858), channel_id=1, source_target_pairs={{0,16},{16,32},{32,48},{48,64},{64,80},{80,96},{96,112},{112,128},... | collective-permute-start | bytes 786440 | tf_op jit(solution)/shard_map/while/body/eval_jaxpr/ppermute | solution.py:13
  406.5 10.1 %collective-permute-start = (bf16[64,2048]{1,0:T(8,128)(2,1)S(1)}, bf16[64,2048]{1,0:T(8,128)(2,1)S(1)}, u32[]{:S(2)}, u32[]{:S(2)}) collective-permute-start(bf16[64,2048]{1,0:T(8,128)(2,1)S(1)} %get-tuple-element.858), channel_id=1, source_target_pairs={{0,16},{16,32},{32,48},{48,64},{64,80},{80,96},{96,112},{112,128},... | collective-permute-start | bytes 786440 | tf_op jit(solution)/shard_map/while/body/eval_jaxpr/ppermute | solution.py:13
  420.2 10.1 %collective-permute-start = (bf16[64,2048]{1,0:T(8,128)(2,1)S(1)}, bf16[64,2048]{1,0:T(8,128)(2,1)S(1)}, u32[]{:S(2)}, u32[]{:S(2)}) collective-permute-start(bf16[64,2048]{1,0:T(8,128)(2,1)S(1)} %get-tuple-element.858), channel_id=1, source_target_pairs={{0,16},{16,32},{32,48},{48,64},{64,80},{80,96},{96,112},{112,128},... | collective-permute-start | bytes 786440 | tf_op jit(solution)/shard_map/while/body/eval_jaxpr/ppermute | solution.py:13
  433.8 10.1 %collective-permute-start = (bf16[64,2048]{1,0:T(8,128)(2,1)S(1)}, bf16[64,2048]{1,0:T(8,128)(2,1)S(1)}, u32[]{:S(2)}, u32[]{:S(2)}) collective-permute-start(bf16[64,2048]{1,0:T(8,128)(2,1)S(1)} %get-tuple-element.858), channel_id=1, source_target_pairs={{0,16},{16,32},{32,48},{48,64},{64,80},{80,96},{96,112},{112,128},... | collective-permute-start | bytes 786440 | tf_op jit(solution)/shard_map/while/body/eval_jaxpr/ppermute | solution.py:13
  447.5 10.1 %collective-permute-start = (bf16[64,2048]{1,0:T(8,128)(2,1)S(1)}, bf16[64,2048]{1,0:T(8,128)(2,1)S(1)}, u32[]{:S(2)}, u32[]{:S(2)}) collective-permute-start(bf16[64,2048]{1,0:T(8,128)(2,1)S(1)} %get-tuple-element.858), channel_id=1, source_target_pairs={{0,16},{16,32},{32,48},{48,64},{64,80},{80,96},{96,112},{112,128},... | collective-permute-start | bytes 786440 | tf_op jit(solution)/shard_map/while/body/eval_jaxpr/ppermute | solution.py:13
  461.1 10.1 %collective-permute-start = (bf16[64,2048]{1,0:T(8,128)(2,1)S(1)}, bf16[64,2048]{1,0:T(8,128)(2,1)S(1)}, u32[]{:S(2)}, u32[]{:S(2)}) collective-permute-start(bf16[64,2048]{1,0:T(8,128)(2,1)S(1)} %get-tuple-element.858), channel_id=1, source_target_pairs={{0,16},{16,32},{32,48},{48,64},{64,80},{80,96},{96,112},{112,128},... | collective-permute-start | bytes 786440 | tf_op jit(solution)/shard_map/while/body/eval_jaxpr/ppermute | solution.py:13
  474.3 10.8 %collective-permute-start.1 = (bf16[64,2048]{1,0:T(8,128)(2,1)S(1)}, bf16[64,2048]{1,0:T(8,128)(2,1)S(1)}, u32[]{:S(2)}, u32[]{:S(2)}) collective-permute-start(bf16[64,2048]{1,0:T(8,128)(2,1)S(1)} %get-tuple-element.876), channel_id=1, source_target_pairs={{16,0},{32,16},{48,32},{64,48},{80,64},{96,80},{112,96},{128,112},... | collective-permute-start | bytes 786440 | tf_op jit(solution)/shard_map/while/body/eval_jaxpr/ppermute | solution.py:13
  487.0 9.2 collective-permute-start.1
  498.1 10.8 %collective-permute-start.1 = (bf16[64,2048]{1,0:T(8,128)(2,1)S(1)}, bf16[64,2048]{1,0:T(8,128)(2,1)S(1)}, u32[]{:S(2)}, u32[]{:S(2)}) collective-permute-start(bf16[64,2048]{1,0:T(8,128)(2,1)S(1)} %get-tuple-element.876), channel_id=1, source_target_pairs={{16,0},{32,16},{48,32},{64,48},{80,64},{96,80},{112,96},{128,112},... | collective-permute-start | bytes 786440 | tf_op jit(solution)/shard_map/while/body/eval_jaxpr/ppermute | solution.py:13
  510.7 10.1 %collective-permute-start.1 = (bf16[64,2048]{1,0:T(8,128)(2,1)S(1)}, bf16[64,2048]{1,0:T(8,128)(2,1)S(1)}, u32[]{:S(2)}, u32[]{:S(2)}) collective-permute-start(bf16[64,2048]{1,0:T(8,128)(2,1)S(1)} %get-tuple-element.876), channel_id=1, source_target_pairs={{16,0},{32,16},{48,32},{64,48},{80,64},{96,80},{112,96},{128,112},... | collective-permute-start | bytes 786440 | tf_op jit(solution)/shard_map/while/body/eval_jaxpr/ppermute | solution.py:13
  522.7 10.1 %collective-permute-start.1 = (bf16[64,2048]{1,0:T(8,128)(2,1)S(1)}, bf16[64,2048]{1,0:T(8,128)(2,1)S(1)}, u32[]{:S(2)}, u32[]{:S(2)}) collective-permute-start(bf16[64,2048]{1,0:T(8,128)(2,1)S(1)} %get-tuple-element.876), channel_id=1, source_target_pairs={{16,0},{32,16},{48,32},{64,48},{80,64},{96,80},{112,96},{128,112},... | collective-permute-start | bytes 786440 | tf_op jit(solution)/shard_map/while/body/eval_jaxpr/ppermute | solution.py:13
  534.7 10.1 %collective-permute-start.1 = (bf16[64,2048]{1,0:T(8,128)(2,1)S(1)}, bf16[64,2048]{1,0:T(8,128)(2,1)S(1)}, u32[]{:S(2)}, u32[]{:S(2)}) collective-permute-start(bf16[64,2048]{1,0:T(8,128)(2,1)S(1)} %get-tuple-element.876), channel_id=1, source_target_pairs={{16,0},{32,16},{48,32},{64,48},{80,64},{96,80},{112,96},{128,112},... | collective-permute-start | bytes 786440 | tf_op jit(solution)/shard_map/while/body/eval_jaxpr/ppermute | solution.py:13
  546.6 10.1 %collective-permute-start.1 = (bf16[64,2048]{1,0:T(8,128)(2,1)S(1)}, bf16[64,2048]{1,0:T(8,128)(2,1)S(1)}, u32[]{:S(2)}, u32[]{:S(2)}) collective-permute-start(bf16[64,2048]{1,0:T(8,128)(2,1)S(1)} %get-tuple-element.876), channel_id=1, source_target_pairs={{16,0},{32,16},{48,32},{64,48},{80,64},{96,80},{112,96},{128,112},... | collective-permute-start | bytes 786440 | tf_op jit(solution)/shard_map/while/body/eval_jaxpr/ppermute | solution.py:13
  558.6 10.1 %collective-permute-start.1 = (bf16[64,2048]{1,0:T(8,128)(2,1)S(1)}, bf16[64,2048]{1,0:T(8,128)(2,1)S(1)}, u32[]{:S(2)}, u32[]{:S(2)}) collective-permute-start(bf16[64,2048]{1,0:T(8,128)(2,1)S(1)} %get-tuple-element.876), channel_id=1, source_target_pairs={{16,0},{32,16},{48,32},{64,48},{80,64},{96,80},{112,96},{128,112},... | collective-permute-start | bytes 786440 | tf_op jit(solution)/shard_map/while/body/eval_jaxpr/ppermute | solution.py:13
  570.5 10.1 %collective-permute-start.1 = (bf16[64,2048]{1,0:T(8,128)(2,1)S(1)}, bf16[64,2048]{1,0:T(8,128)(2,1)S(1)}, u32[]{:S(2)}, u32[]{:S(2)}) collective-permute-start(bf16[64,2048]{1,0:T(8,128)(2,1)S(1)} %get-tuple-element.876), channel_id=1, source_target_pairs={{16,0},{32,16},{48,32},{64,48},{80,64},{96,80},{112,96},{128,112},... | collective-permute-start | bytes 786440 | tf_op jit(solution)/shard_map/while/body/eval_jaxpr/ppermute | solution.py:13
  582.5 10.1 %collective-permute-start.1 = (bf16[64,2048]{1,0:T(8,128)(2,1)S(1)}, bf16[64,2048]{1,0:T(8,128)(2,1)S(1)}, u32[]{:S(2)}, u32[]{:S(2)}) collective-permute-start(bf16[64,2048]{1,0:T(8,128)(2,1)S(1)} %get-tuple-element.876), channel_id=1, source_target_pairs={{16,0},{32,16},{48,32},{64,48},{80,64},{96,80},{112,96},{128,112},... | collective-permute-start | bytes 786440 | tf_op jit(solution)/shard_map/while/body/eval_jaxpr/ppermute | solution.py:13
  594.5 10.1 %collective-permute-start.1 = (bf16[64,2048]{1,0:T(8,128)(2,1)S(1)}, bf16[64,2048]{1,0:T(8,128)(2,1)S(1)}, u32[]{:S(2)}, u32[]{:S(2)}) collective-permute-start(bf16[64,2048]{1,0:T(8,128)(2,1)S(1)} %get-tuple-element.876), channel_id=1, source_target_pairs={{16,0},{32,16},{48,32},{64,48},{80,64},{96,80},{112,96},{128,112},... | collective-permute-start | bytes 786440 | tf_op jit(solution)/shard_map/while/body/eval_jaxpr/ppermute | solution.py:13
  606.4 10.1 %collective-permute-start.1 = (bf16[64,2048]{1,0:T(8,128)(2,1)S(1)}, bf16[64,2048]{1,0:T(8,128)(2,1)S(1)}, u32[]{:S(2)}, u32[]{:S(2)}) collective-permute-start(bf16[64,2048]{1,0:T(8,128)(2,1)S(1)} %get-tuple-element.876), channel_id=1, source_target_pairs={{16,0},{32,16},{48,32},{64,48},{80,64},{96,80},{112,96},{128,112},... | collective-permute-start | bytes 786440 | tf_op jit(solution)/shard_map/while/body/eval_jaxpr/ppermute | solution.py:13
  618.4 10.1 %collective-permute-start.1 = (bf16[64,2048]{1,0:T(8,128)(2,1)S(1)}, bf16[64,2048]{1,0:T(8,128)(2,1)S(1)}, u32[]{:S(2)}, u32[]{:S(2)}) collective-permute-start(bf16[64,2048]{1,0:T(8,128)(2,1)S(1)} %get-tuple-element.876), channel_id=1, source_target_pairs={{16,0},{32,16},{48,32},{64,48},{80,64},{96,80},{112,96},{128,112},... | collective-permute-start | bytes 786440 | tf_op jit(solution)/shard_map/while/body/eval_jaxpr/ppermute | solution.py:13
  630.3 64.2 %collective-permute-start.1 = (bf16[64,2048]{1,0:T(8,128)(2,1)S(1)}, bf16[64,2048]{1,0:T(8,128)(2,1)S(1)}, u32[]{:S(2)}, u32[]{:S(2)}) collective-permute-start(bf16[64,2048]{1,0:T(8,128)(2,1)S(1)} %get-tuple-element.876), channel_id=1, source_target_pairs={{16,0},{32,16},{48,32},{64,48},{80,64},{96,80},{112,96},{128,112},... | collective-permute-start | bytes 786440 | tf_op jit(solution)/shard_map/while/body/eval_jaxpr/ppermute | solution.py:13
  704.1 10.1 %collective-permute-start.1 = (bf16[64,2048]{1,0:T(8,128)(2,1)S(1)}, bf16[64,2048]{1,0:T(8,128)(2,1)S(1)}, u32[]{:S(2)}, u32[]{:S(2)}) collective-permute-start(bf16[64,2048]{1,0:T(8,128)(2,1)S(1)} %get-tuple-element.876), channel_id=1, source_target_pairs={{16,0},{32,16},{48,32},{64,48},{80,64},{96,80},{112,96},{128,112},... | collective-permute-start | bytes 786440 | tf_op jit(solution)/shard_map/while/body/eval_jaxpr/ppermute | solution.py:13
  723.7 10.1 %collective-permute-start.1 = (bf16[64,2048]{1,0:T(8,128)(2,1)S(1)}, bf16[64,2048]{1,0:T(8,128)(2,1)S(1)}, u32[]{:S(2)}, u32[]{:S(2)}) collective-permute-start(bf16[64,2048]{1,0:T(8,128)(2,1)S(1)} %get-tuple-element.876), channel_id=1, source_target_pairs={{16,0},{32,16},{48,32},{64,48},{80,64},{96,80},{112,96},{128,112},... | collective-permute-start | bytes 786440 | tf_op jit(solution)/shard_map/while/body/eval_jaxpr/ppermute | solution.py:13
  743.3 10.1 %collective-permute-start.1 = (bf16[64,2048]{1,0:T(8,128)(2,1)S(1)}, bf16[64,2048]{1,0:T(8,128)(2,1)S(1)}, u32[]{:S(2)}, u32[]{:S(2)}) collective-permute-start(bf16[64,2048]{1,0:T(8,128)(2,1)S(1)} %get-tuple-element.876), channel_id=1, source_target_pairs={{16,0},{32,16},{48,32},{64,48},{80,64},{96,80},{112,96},{128,112},... | collective-permute-start | bytes 786440 | tf_op jit(solution)/shard_map/while/body/eval_jaxpr/ppermute | solution.py:13
  762.9 9.2 collective-permute-start.1
  774.0 9.2 collective-permute-start.1
  790.3 0.7 copy-start
Sparse Core Ops, SparseCore 0:
  9.8 187.6 all-gather.1
  790.4 180.5 reduce-scatter.1
where the time goes:
time: 986 us; the launch traced here: 981 us
  waiting for transfers between devices  461 us (47%)
  starting transfers between devices  158 us (16%)
  other arithmetic  112 us (11%)
  blocking collectives  94.8 us (10%)
  local copies, waits for them, and re-layouts  83.8 us (8%)
  matrix products  52.5 us (5%)
  between operations  16.5 us (2%)
    ppermute x38, waiting for transfers between devices, passed_along(): return lax.ppermute(block, axis, route)  191 us
    ppermute x38, starting transfers between devices, passed_along(): return lax.ppermute(block, axis, route)  158 us
    reduce_scatter x1, waiting for transfers between devices, local(): lax.psum_scatter(weight_total.astype(jnp.bfloat16), 'fsdp', scatter_dimen...  144 us
    all_gather x1, waiting for transfers between devices, local(): lax.all_gather(section_weights, 'fsdp', axis=1, tiled=True)  126 us
    dynamic_update_slice x95, other arithmetic, store_slot(): return lax.dynamic_update_index_in_dim(buffer, chosen, position, 0)  72.9 us
    dynamic_slice x76, local copies, waits for them, and re-layouts, store_slot(): previous = lax.dynamic_index_in_dim(buffer, position, 0, keepdims=False)  56.2 us
    unnamed x1, blocking collectives  34.5 us
    all_gather x1, blocking collectives, local(): lax.all_gather(section_gains, 'fsdp', axis=1, tiled=True)  33 us
  transfers between devices with their start and end apart: 40, of which 40 were waited for; matrix products, arithmetic and copies ran while one was open for 8% of the time, Pallas kernels for 0%

commit v1 on v0

v1 whole, which is shorter than its diff:
```python
import functools

import jax
import jax.numpy as jnp
from jax import lax
from jax.experimental import pallas as pl
from jax.experimental.pallas import tpu as pltpu
from jax.sharding import PartitionSpec as P

clip_epsilon = 0.2
norm_epsilon = 1e-05
SPLIT = 1
BLOCK = 512
f32 = jnp.float32
bf16 = jnp.bfloat16


def vmem():
    return pl.BlockSpec(memory_space=pltpu.VMEM)


def params(mib):
    return pltpu.CompilerParams(vmem_limit_bytes=mib << 20)


def from_z_below(value):
    n = lax.axis_size("fsdp")
    return lax.ppermute(value, "fsdp", [(i, (i + 2) % n) for i in range(n)])


def from_z_above(value):
    n = lax.axis_size("fsdp")
    return lax.ppermute(value, "fsdp", [(i, (i - 2) % n) for i in range(n)])


def from_x(value):
    n = lax.axis_size("fsdp")
    return lax.ppermute(value, "fsdp", [(i, i ^ 1) for i in range(n)])


def from_partner(value, distance):
    n = lax.axis_size("fsdp")
    return lax.ppermute(value, "fsdp", [(i, i ^ distance) for i in range(n)])


GATHER = (
    ((0, 0), "zp", (-1, 0)),
    ((0, 0), "zm", (1, 0)),
    ((0, 0), "x", (0, 1)),
    ((-1, 0), "zp", (-2, 0)),
    ((1, 0), "zm", (2, 0)),
    ((-1, 0), "x", (-1, 1)),
    ((-2, 0), "zp", (-3, 0)),
    ((2, 0), "zm", (3, 0)),
    ((1, 0), "x", (1, 1)),
    ((-1, 1), "zp", (-2, 1)),
    ((1, 1), "zm", (2, 1)),
    ((-3, 0), "x", (-3, 1)),
    ((-3, 1), "zp", (-4, 1)),
    ((3, 0), "zm", (4, 0)),
    ((3, 0), "x", (3, 1)),
)
MOVE = {"zp": from_z_below, "zm": from_z_above, "x": from_x}
BACK = {"zp": from_z_above, "zm": from_z_below, "x": from_x}
KEYS = ((0, 0),) + tuple(entry[2] for entry in GATHER)


def shard_index(key):
    n = lax.axis_size("fsdp")
    me = lax.axis_index("fsdp")
    owner_z = lax.rem(me // 2 + key[0] + n // 2, n // 2)
    owner_a = lax.rem(lax.rem(me, 2) + key[1], 2)
    return owner_z * 2 + owner_a


def forward_kernel(tick, count, first, *refs):
    if first:
        fresh, matrix, gain, out, h_all, n_all, d_all, r_all, turned = refs
        incoming = None
    else:
        if tick < count:
            fresh, incoming, matrix, gain = refs[:4]
        else:
            incoming, matrix, gain = refs[:3]
        out, h_all, n_all, d_all, r_all, turned = refs[-6:]
    mine = lax.axis_index("section")
    slot = tick - mine
    live = (slot >= 0) & (slot < count)
    width = matrix.shape[0]

    def run(source, where):
        h = source[...].astype(f32)
        scale = lax.rsqrt(jnp.mean(h * h, axis=-1, keepdims=True) + norm_epsilon)
        n_all[where] = (h * scale * gain[...]).astype(bf16)
        h_all[where] = source[...]
        r_all[where] = jnp.broadcast_to(scale, r_all.shape[1:])
        for c in range(0, width, BLOCK):
            cols = slice(c, c + BLOCK)
            p = jnp.dot(n_all[where], matrix[:, cols], preferred_element_type=f32)
            gate = jax.nn.sigmoid(p)
            out[:, cols] = (source[:, cols].astype(f32) + p * gate).astype(bf16)
            d_all[where, :, cols] = gate * (1.0 + p * (1.0 - gate))

    if tick < count:
        @pl.when(mine == 0)
        def _():
            run(fresh.at[tick], tick)

    if not first:
        @pl.when(live & (mine > 0))
        def _():
            run(incoming, slot)

    idle = jnp.where(slot < 0, tick, tick - count)
    pieces = 8
    rows = width // pieces

    @pl.when(jnp.logical_not(live) & (idle < pieces))
    def _():
        at = pl.multiple_of(idle * rows, rows)
        for c in range(0, width, BLOCK):
            turned[c : c + BLOCK, pl.ds(at, rows)] = matrix[pl.ds(at, rows), c : c + BLOCK].T


def forward_tick(tick, count, fresh, incoming, matrix, gain, kept):
    rows, width = fresh.shape[1:]
    first = tick == 0
    operands = []
    if tick < count:
        operands.append(fresh)
    if not first:
        operands.append(incoming)
    operands += [matrix, gain]
    shapes = [
        jax.ShapeDtypeStruct((rows, width), bf16),
        jax.ShapeDtypeStruct((count, rows, width), bf16),
        jax.ShapeDtypeStruct((count, rows, width), bf16),
        jax.ShapeDtypeStruct((count, rows, width), f32),
        jax.ShapeDtypeStruct((count, rows, 128), f32),
        jax.ShapeDtypeStruct((width, width), bf16),
    ]
    aliases = {}
    if not first:
        aliases = {len(operands) + i: 1 + i for i in range(5)}
        operands += list(kept)
    results = pl.pallas_call(
        functools.partial(forward_kernel, tick, count, first),
        in_specs=[vmem()] * len(operands),
        out_specs=[vmem()] * 6,
        out_shape=shapes,
        input_output_aliases=aliases,
        compiler_params=params(24),
        name=f"forward_layer_{tick}",
    )(*operands)
    return results[0], tuple(results[1:])


def backward_kernel(tick, count, sections, first, *refs):
    if first:
        top, turned, gain, h_all, d_all, r_all, out, p_all, gain_sum, wide = refs
        incoming = None
    else:
        if tick < count:
            top, incoming, turned, gain, h_all, d_all, r_all = refs[:7]
        else:
            incoming, turned, gain, h_all, d_all, r_all = refs[:6]
        out, p_all, gain_sum, wide = refs[-4:]
    mine = lax.axis_index("section")
    slot = tick - (sections - 1 - mine)
    live = (slot >= 0) & (slot < count)
    width = turned.shape[0]

    def run(source, where):
        p_all[where] = (source[...].astype(f32) * d_all[where]).astype(bf16)
        scale = r_all[where][:, :1]
        dots = jnp.zeros((source.shape[0], 1), f32)
        for c in range(0, width, BLOCK):
            cols = slice(c, c + BLOCK)
            ng = jnp.dot(p_all[where], turned[:, cols], preferred_element_type=f32)
            h = h_all[where, :, cols].astype(f32)
            gain_rows = jnp.sum(ng * h * scale, axis=0, keepdims=True)
            gain_sum[:, cols] = jnp.where(where == 0, 0.0, gain_sum[:, cols]) + gain_rows
            scaled = gain[:, cols] * ng
            wide[:, cols] = scaled
            dots = dots + jnp.sum(scaled * h, axis=-1, keepdims=True)
        factor = scale * scale * scale * (dots / width)
        for c in range(0, width, BLOCK):
            cols = slice(c, c + BLOCK)
            h = h_all[where, :, cols].astype(f32)
            g = source[:, cols].astype(f32)
            out[:, cols] = (g + (scale * wide[:, cols] - h * factor)).astype(bf16)

    if tick < count:
        @pl.when(mine == sections - 1)
        def _():
            run(top.at[tick], tick)

    if not first:
        @pl.when(live & (mine < sections - 1))
        def _():
            run(incoming, slot)


def backward_tick(tick, count, sections, top, incoming, turned, gain, kept, grads):
    rows, width = top.shape[1:]
    first = tick == 0
    operands = []
    if tick < count:
        operands.append(top)
    if not first:
        operands.append(incoming)
    operands += [turned, gain, kept[0], kept[2], kept[3]]
    shapes = [
        jax.ShapeDtypeStruct((rows, width), bf16),
        jax.ShapeDtypeStruct((count, rows, width), bf16),
        jax.ShapeDtypeStruct((1, width), f32),
    ]
    aliases = {}
    if not first:
        aliases = {len(operands) + i: 1 + i for i in range(2)}
        operands += list(grads)
    results = pl.pallas_call(
        functools.partial(backward_kernel, tick, count, sections, first),
        in_specs=[vmem()] * len(operands),
        out_specs=[vmem()] * 3,
        out_shape=shapes,
        input_output_aliases=aliases,
        scratch_shapes=[pltpu.VMEM((rows, width), f32)],
        compiler_params=params(24),
        name=f"backward_layer_{tick}",
    )(*operands)
    return results[0], tuple(results[1:])


def weight_kernel(normed, grad, *outs):
    rows = outs[0].shape[0]
    width = grad.shape[1]
    for key, out in zip(KEYS, outs):
        at = pl.multiple_of(shard_index(key) * rows, rows)
        left = normed[:, pl.ds(at, rows)]
        for c in range(0, width, BLOCK):
            cols = slice(c, c + BLOCK)
            out[:, cols] = lax.dot_general(
                left, grad[:, cols], (((0,), (0,)), ((), ())), preferred_element_type=f32
            ).astype(bf16)


def weight_partials(normed, grad, shards):
    width = grad.shape[1]
    rows = width // shards
    return pl.pallas_call(
        weight_kernel,
        in_specs=[vmem(), vmem()],
        out_specs=[vmem()] * shards,
        out_shape=[jax.ShapeDtypeStruct((rows, width), bf16)] * shards,
        compiler_params=params(16),
        name="weight_partials",
    )(normed, grad)


def assemble_kernel(shards, *refs):
    pieces = refs[:shards]
    fresh, top, matrix, fresh_out, top_out, sems = refs[shards:]
    rows = pieces[0].shape[0]
    copies = [
        pltpu.make_async_copy(fresh, fresh_out, sems.at[shards]),
        pltpu.make_async_copy(top, top_out, sems.at[shards + 1]),
    ]
    for i, (key, piece) in enumerate(zip(KEYS, pieces)):
        at = pl.multiple_of(shard_index(key) * rows, rows)
        copies.append(pltpu.make_async_copy(piece, matrix.at[pl.ds(at, rows)], sems.at[i]))
    for copy in copies:
        copy.start()
    for copy in copies:
        copy.wait()


def assemble(pieces, fresh, top):
    shards = len(pieces)
    rows, width = pieces[0].shape
    return pl.pallas_call(
        functools.partial(assemble_kernel, shards),
        in_specs=[pl.BlockSpec(memory_space=pl.ANY)] * (shards + 2),
        out_specs=[vmem()] * 3,
        out_shape=[
            jax.ShapeDtypeStruct((shards * rows, width), bf16),
            jax.ShapeDtypeStruct(fresh.shape, bf16),
            jax.ShapeDtypeStruct(top.shape, bf16),
        ],
        scratch_shapes=[pltpu.SemaphoreType.DMA((shards + 2,))],
        compiler_params=params(12),
        name="assemble",
    )(*pieces, fresh, top)


def add_kernel(*refs):
    out = refs[-1]
    acc = refs[0][...].astype(f32)
    for ref in refs[1:-1]:
        acc = acc + ref[...].astype(f32)
    out[...] = acc.astype(out.dtype)


def add(*values, kind=None):
    return pl.pallas_call(
        add_kernel,
        in_specs=[vmem()] * len(values),
        out_specs=vmem(),
        out_shape=jax.ShapeDtypeStruct(values[0].shape, kind or values[0].dtype),
        compiler_params=params(8),
        name="add",
    )(*values)


def local(
    embeddings,
    section_weights,
    section_gains,
    top_direction,
    new_logprob,
    old_logprob,
    segment_ids,
    advantages,
):
    sections = lax.axis_size("section")
    shards = lax.axis_size("fsdp")
    shard = lax.axis_index("fsdp")
    micro_batches, row_count, width = embeddings.shape
    seq_count = advantages.shape[1]
    count = micro_batches * SPLIT
    rows = row_count // SPLIT
    share = width // shards

    labels = lax.broadcasted_iota(jnp.int32, (1, 1, seq_count), 2)
    member = (segment_ids[:, :, None] == labels).astype(f32)
    log_drift = new_logprob - old_logprob
    part_sums = jnp.sum(log_drift[:, :, None] * member, axis=1)
    part_counts = jnp.sum(member, axis=1)
    spread = jnp.zeros((1, width), f32)
    spread = lax.dynamic_update_slice(spread, section_gains.astype(f32), (0, shard * share))
    table = micro_batches * seq_count
    small = jnp.concatenate(
        [spread, part_sums.reshape(1, table), part_counts.reshape(1, table),
         jnp.zeros((1, 128 - 2 * table), f32)], axis=1
    )

    held = {(0, 0): section_weights[0]}
    distance = 1
    for i, (sent, move, got) in enumerate(GATHER):
        held[got] = MOVE[move](held[sent])
        if i % 3 == 2 and distance < shards:
            small = add(small, from_partner(small, distance))
            distance *= 2

    gain = small[:, :width]
    seq_sums = small[:, width : width + table].reshape(micro_batches, seq_count)
    seq_counts = small[:, width + table : width + 2 * table].reshape(micro_batches, seq_count)
    seq_ratio = jnp.exp(seq_sums / seq_counts)
    clipped = jnp.clip(seq_ratio, 1.0 - clip_epsilon, 1.0 + clip_epsilon)
    plain_term = seq_ratio * advantages
    bounded_term = clipped * advantages
    gspo_loss = -jnp.sum(jnp.minimum(plain_term, bounded_term))
    per_seq = jnp.where(plain_term <= bounded_term, -advantages * seq_ratio / seq_counts, 0.0)
    token_coef = jnp.sum(member * per_seq[:, None, :], axis=2)
    top_grad = (token_coef[:, :, None] * top_direction.astype(f32)).astype(bf16)
    top_grad = top_grad.reshape(count, rows, width)
    fresh = embeddings.reshape(count, rows, width)
    pieces = [held[key] for key in KEYS]
    pieces, fresh, top_grad, gain, gspo_loss = lax.optimization_barrier(
        (pieces, fresh, top_grad, gain, gspo_loss)
    )
    matrix, fresh, top_grad = assemble(pieces, fresh, top_grad)

    ticks = count + sections - 1
    state, kept = None, None
    for tick in range(ticks):
        state, kept = forward_tick(tick, count, fresh, state, matrix, gain, kept)
        route = [(s, s + 1) for s in range(sections - 1) if 0 <= tick - s < count]
        if route:
            state = lax.ppermute(state, "section", route)

    state, grads = None, None
    for tick in range(ticks):
        state, grads = backward_tick(
            tick, count, sections, top_grad, state, kept[4], gain, kept, grads
        )
        route = [
            (s, s - 1) for s in range(1, sections) if 0 <= tick - (sections - 1 - s) < count
        ]
        if route:
            state = lax.ppermute(state, "section", route)

    tokens = count * rows
    partials = weight_partials(
        kept[1].reshape(tokens, width), grads[0].reshape(tokens, width), shards
    )
    total = dict(zip(KEYS, partials))
    gain_total = add(grads[1], kind=bf16)
    distance = 1
    back = tuple(reversed(GATHER))
    for step in range(0, len(back), 3):
        came = {}
        for home, move, far in back[step : step + 3]:
            came.setdefault(home, []).append(BACK[move](total.pop(far)))
        if distance < shards:
            gain_total = add(gain_total, from_partner(gain_total, distance), kind=f32)
            distance *= 2
        for home, values in came.items():
            total[home] = add(total[home], *values, kind=f32 if home == (0, 0) else bf16)
    gain_share = lax.dynamic_slice(gain_total, (0, shard * share), (1, share))
    return (total[0, 0][None], gain_share, gspo_loss)


def solution(mesh):
    placed = (
        P(None, "fsdp", None),
        P("section", "fsdp", None),
        P("section", "fsdp"),
        P(None, "fsdp", None),
        P(None, "fsdp"),
        P(None, "fsdp"),
        P(None, "fsdp"),
        P(),
    )
    return jax.shard_map(
        local,
        mesh=mesh,
        in_specs=placed,
        out_specs=(P("section", "fsdp", None), P("section", "fsdp"), P()),
        check_vma=False,
    )
```

time: 986 us -> 630 us (0.64)
  the two profiles are of different devices: /device:TPU:1 before, /device:TPU:2 now
where the time goes in v1:
time: 630 us; the launch traced here: 620 us
  starting transfers between devices  384 us (61%)
  waiting for transfers between devices  195 us (31%)
  Pallas kernels  28.9 us (5%)
    ppermute x36, starting transfers between devices, local(): state = lax.ppermute(state, 'section', route)  316 us
    ppermute x36, waiting for transfers between devices, local(): state = lax.ppermute(state, 'section', route)  80.5 us
    ppermute x10, waiting for transfers between devices, from_z_below(): return lax.ppermute(value, 'fsdp', [(i, (i + 2) % n) for i in range(n)])  44.1 us
    ppermute x10, waiting for transfers between devices, from_x(): return lax.ppermute(value, 'fsdp', [(i, i ^ 1) for i in range(n)])  34.3 us
    ppermute x10, starting transfers between devices, from_z_above(): return lax.ppermute(value, 'fsdp', [(i, (i - 2) % n) for i in range(n)])  32.5 us
    ppermute x8, waiting for transfers between devices, from_partner(): return lax.ppermute(value, 'fsdp', [(i, i ^ distance) for i in range(n)])  26.9 us
    ppermute x10, starting transfers between devices, from_x(): return lax.ppermute(value, 'fsdp', [(i, i ^ 1) for i in range(n)])  17.2 us
  transfers between devices with their start and end apart: 74, of which 31 were waited for; matrix products, arithmetic and copies ran while one was open for 1% of the time, Pallas kernels for 0%

profile of v1, /device:TPU:2, one launch (start us, length us, event | category | flops | bytes accessed | tf_op | source)
XLA Modules:
  0.0 620.4 jit_solution(6466960020385066145)
XLA Ops:
  2.6 4.0 collective-permute-start.1
  6.7 12.0 %collective-permute-done.refs_1_ = bf16[128,2048]{1,0:T(8,128)(2,1)S(1)} collective-permute-done((bf16[128,2048]{1,0:T(8,128)(2,1)}, bf16[128,2048]{1,0:T(8,128)(2,1)S(1)}, u32[]{:S(2)}, u32[]{:S(2)}) %collective-permute-start) | collective-permute-done | bytes 524320 | tf_op jit(solution)/shard_map/ppermute | solution.py:28
  18.7 3.2 collective-permute-start.4
  22.0 11.1 %collective-permute-done.3.refs_4_ = bf16[128,2048]{1,0:T(8,128)(2,1)S(1)} collective-permute-done((bf16[128,2048]{1,0:T(8,128)(2,1)S(1)}, bf16[128,2048]{1,0:T(8,128)(2,1)S(1)}, u32[]{:S(2)}, u32[]{:S(2)}) %collective-permute-start.3) | collective-permute-done | bytes 524320 | tf_op jit(solution)/shard_map/ppermute | solution.py:28
  36.1 3.1 collective-permute-done.15.refs_1_
  39.2 4.1 collective-permute-done.16.refs_1_
  43.3 2.6 collective-permute-start.17
  47.9 3.6 collective-permute-start.18
  53.6 3.1 collective-permute-start.7
  57.2 10.0 %collective-permute-start.11 = (bf16[128,2048]{1,0:T(8,128)(2,1)}, bf16[128,2048]{1,0:T(8,128)(2,1)}, u32[]{:S(2)}, u32[]{:S(2)}) collective-permute-start(bf16[128,2048]{1,0:T(8,128)(2,1)} %collective-permute-done.6.refs_7_), channel_id=1, source_target_pairs={{0,1},{1,0},{2,3},{3,2},{4,5},{5,4},{6,7},{7,6},{8,9},{9,8},{10,11... | collective-permute-start | bytes 1572872 | tf_op jit(solution)/shard_map/ppermute | solution.py:38
  68.7 4.4 collective-permute-start.10
  73.2 4.6 collective-permute-done.5.refs_6_
  77.7 2.5 collective-permute-start.9
  80.8 8.2 %collective-permute-done.2.refs_3_ = bf16[128,2048]{1,0:T(8,128)(2,1)} collective-permute-done((bf16[128,2048]{1,0:T(8,128)(2,1)}, bf16[128,2048]{1,0:T(8,128)(2,1)}, u32[]{:S(2)}, u32[]{:S(2)}) %collective-permute-start.2) | collective-permute-done | bytes 524320 | tf_op jit(solution)/shard_map/ppermute | solution.py:38
  89.0 3.1 collective-permute-start.13
  92.0 8.2 %collective-permute-done.11.refs_12_ = bf16[128,2048]{1,0:T(8,128)(2,1)} collective-permute-done((bf16[128,2048]{1,0:T(8,128)(2,1)}, bf16[128,2048]{1,0:T(8,128)(2,1)}, u32[]{:S(2)}, u32[]{:S(2)}) %collective-permute-start.11) | collective-permute-done | bytes 524320 | tf_op jit(solution)/shard_map/ppermute | solution.py:38
  100.2 2.7 collective-permute-start.12
  106.7 4.4 collective-permute-done.12.refs_13_
  113.2 3.2 assemble.1
  127.5 4.1 collective-permute-start.21
  134.5 8.0 %collective-permute-start.22 = (bf16[64,2048]{1,0:T(8,128)(2,1)S(1)}, bf16[64,2048]{1,0:T(8,128)(2,1)S(1)}, u32[]{:S(2)}, u32[]{:S(2)}) collective-permute-start(bf16[64,2048]{1,0:T(8,128)(2,1)S(1)} %get-tuple-element.250), channel_id=1, source_target_pairs={{0,16},{16,32},{32,48},{48,64},{1,17},{17,33},{33,49},{49,65},{2,1... | collective-permute-start | bytes 786440 | tf_op jit(solution)/shard_map/ppermute | solution.py:380
  150.9 54.9 %collective-permute-start.29 = (bf16[64,2048]{1,0:T(8,128)(2,1)S(1)}, bf16[64,2048]{1,0:T(8,128)(2,1)S(1)}, u32[]{:S(2)}, u32[]{:S(2)}) collective-permute-start(bf16[64,2048]{1,0:T(8,128)(2,1)S(1)} %get-tuple-element.292), channel_id=1, source_target_pairs={{112,128},{128,144},{144,160},{160,176},{113,129},{129,145},{145,1... | collective-permute-start | bytes 786440 | tf_op jit(solution)/shard_map/ppermute | solution.py:380
  206.3 19.4 %collective-permute-start.30 = (bf16[64,2048]{1,0:T(8,128)(2,1)S(1)}, bf16[64,2048]{1,0:T(8,128)(2,1)S(1)}, u32[]{:S(2)}, u32[]{:S(2)}) collective-permute-start(bf16[64,2048]{1,0:T(8,128)(2,1)S(1)} %get-tuple-element.298), channel_id=1, source_target_pairs={{128,144},{144,160},{160,176},{176,192},{129,145},{145,161},{161,1... | collective-permute-start | bytes 786440 | tf_op jit(solution)/shard_map/ppermute | solution.py:380
  225.8 19.8 %collective-permute-start.31 = (bf16[64,2048]{1,0:T(8,128)(2,1)S(1)}, bf16[64,2048]{1,0:T(8,128)(2,1)S(1)}, u32[]{:S(2)}, u32[]{:S(2)}) collective-permute-start(bf16[64,2048]{1,0:T(8,128)(2,1)S(1)} %get-tuple-element.304), channel_id=1, source_target_pairs={{144,160},{160,176},{176,192},{192,208},{145,161},{161,177},{177,1... | collective-permute-start | bytes 786440 | tf_op jit(solution)/shard_map/ppermute | solution.py:380
  245.6 19.8 %collective-permute-start.32 = (bf16[64,2048]{1,0:T(8,128)(2,1)S(1)}, bf16[64,2048]{1,0:T(8,128)(2,1)S(1)}, u32[]{:S(2)}, u32[]{:S(2)}) collective-permute-start(bf16[64,2048]{1,0:T(8,128)(2,1)S(1)} %get-tuple-element.310), channel_id=1, source_target_pairs={{160,176},{176,192},{192,208},{208,224},{161,177},{177,193},{193,2... | collective-permute-start | bytes 786440 | tf_op jit(solution)/shard_map/ppermute | solution.py:380
  265.4 19.5 %collective-permute-start.33 = (bf16[64,2048]{1,0:T(8,128)(2,1)S(1)}, bf16[64,2048]{1,0:T(8,128)(2,1)S(1)}, u32[]{:S(2)}, u32[]{:S(2)}) collective-permute-start(bf16[64,2048]{1,0:T(8,128)(2,1)S(1)} %get-tuple-element.316), channel_id=1, source_target_pairs={{176,192},{192,208},{208,224},{224,240},{177,193},{193,209},{209,2... | collective-permute-start | bytes 786440 | tf_op jit(solution)/shard_map/ppermute | solution.py:380
  290.2 67.2 %collective-permute-start.40 = (bf16[64,2048]{1,0:T(8,128)(2,1)S(1)}, bf16[64,2048]{1,0:T(8,128)(2,1)S(1)}, u32[]{:S(2)}, u32[]{:S(2)}) collective-permute-start(bf16[64,2048]{1,0:T(8,128)(2,1)S(1)} %get-tuple-element.355), channel_id=1, source_target_pairs={{192,176},{208,192},{224,208},{240,224},{193,177},{209,193},{225,2... | collective-permute-start | bytes 786440 | tf_op jit(solution)/shard_map/ppermute | solution.py:391
  357.5 20.5 %collective-permute-start.41 = (bf16[64,2048]{1,0:T(8,128)(2,1)S(1)}, bf16[64,2048]{1,0:T(8,128)(2,1)S(1)}, u32[]{:S(2)}, u32[]{:S(2)}) collective-permute-start(bf16[64,2048]{1,0:T(8,128)(2,1)S(1)} %get-tuple-element.358), channel_id=1, source_target_pairs={{176,160},{192,176},{208,192},{224,208},{177,161},{193,177},{209,1... | collective-permute-start | bytes 786440 | tf_op jit(solution)/shard_map/ppermute | solution.py:391
  378.5 20.5 %collective-permute-start.42 = (bf16[64,2048]{1,0:T(8,128)(2,1)S(1)}, bf16[64,2048]{1,0:T(8,128)(2,1)S(1)}, u32[]{:S(2)}, u32[]{:S(2)}) collective-permute-start(bf16[64,2048]{1,0:T(8,128)(2,1)S(1)} %get-tuple-element.361), channel_id=1, source_target_pairs={{160,144},{176,160},{192,176},{208,192},{161,145},{177,161},{193,1... | collective-permute-start | bytes 786440 | tf_op jit(solution)/shard_map/ppermute | solution.py:391
  399.0 20.5 %collective-permute-start.43 = (bf16[64,2048]{1,0:T(8,128)(2,1)S(1)}, bf16[64,2048]{1,0:T(8,128)(2,1)S(1)}, u32[]{:S(2)}, u32[]{:S(2)}) collective-permute-start(bf16[64,2048]{1,0:T(8,128)(2,1)S(1)} %get-tuple-element.364), channel_id=1, source_target_pairs={{144,128},{160,144},{176,160},{192,176},{145,129},{161,145},{177,1... | collective-permute-start | bytes 786440 | tf_op jit(solution)/shard_map/ppermute | solution.py:391
  419.6 20.5 %collective-permute-start.44 = (bf16[64,2048]{1,0:T(8,128)(2,1)S(1)}, bf16[64,2048]{1,0:T(8,128)(2,1)S(1)}, u32[]{:S(2)}, u32[]{:S(2)}) collective-permute-start(bf16[64,2048]{1,0:T(8,128)(2,1)S(1)} %get-tuple-element.367), channel_id=1, source_target_pairs={{128,112},{144,128},{160,144},{176,160},{129,113},{145,129},{161,1... | collective-permute-start | bytes 786440 | tf_op jit(solution)/shard_map/ppermute | solution.py:391
  446.0 51.1 %collective-permute-done.51.refs_0_ = bf16[64,2048]{1,0:T(8,128)(2,1)S(1)} collective-permute-done((bf16[64,2048]{1,0:T(8,128)(2,1)S(1)}, bf16[64,2048]{1,0:T(8,128)(2,1)S(1)}, u32[]{:S(2)}, u32[]{:S(2)}) %collective-permute-start.51) | collective-permute-done | bytes 262176 | tf_op jit(solution)/shard_map/ppermute | solution.py:391
  500.2 8.8 %collective-permute-done.52.refs_0_ = bf16[64,2048]{1,0:T(8,128)(2,1)S(1)} collective-permute-done((bf16[64,2048]{1,0:T(8,128)(2,1)S(1)}, bf16[64,2048]{1,0:T(8,128)(2,1)S(1)}, u32[]{:S(2)}, u32[]{:S(2)}) %collective-permute-start.52) | collective-permute-done | bytes 262176 | tf_op jit(solution)/shard_map/ppermute | solution.py:391
  512.2 8.8 %collective-permute-done.53.refs_0_ = bf16[64,2048]{1,0:T(8,128)(2,1)S(1)} collective-permute-done((bf16[64,2048]{1,0:T(8,128)(2,1)S(1)}, bf16[64,2048]{1,0:T(8,128)(2,1)S(1)}, u32[]{:S(2)}, u32[]{:S(2)}) %collective-permute-start.53) | collective-permute-done | bytes 262176 | tf_op jit(solution)/shard_map/ppermute | solution.py:391
  524.2 7.3 %collective-permute-done.54.refs_0_ = bf16[64,2048]{1,0:T(8,128)(2,1)S(1)} collective-permute-done((bf16[64,2048]{1,0:T(8,128)(2,1)S(1)}, bf16[64,2048]{1,0:T(8,128)(2,1)S(1)}, u32[]{:S(2)}, u32[]{:S(2)}) %collective-permute-start.54) | collective-permute-done | bytes 262176 | tf_op jit(solution)/shard_map/ppermute | solution.py:391
  531.5 2.6 backward_layer_18.1
  536.5 5.3 collective-permute-start.65
  542.1 9.3 %collective-permute-done.65.refs_1_ = bf16[128,2048]{1,0:T(8,128)(2,1)S(1)} collective-permute-done((bf16[128,2048]{1,0:T(8,128)(2,1)S(1)}, bf16[128,2048]{1,0:T(8,128)(2,1)S(1)}, u32[]{:S(2)}, u32[]{:S(2)}) %collective-permute-start.65) | collective-permute-done | bytes 524320 | tf_op jit(solution)/shard_map/ppermute | solution.py:33
  552.2 3.3 collective-permute-start.63
  556.8 8.2 %collective-permute-done.66.refs_1_ = bf16[128,2048]{1,0:T(8,128)(2,1)S(1)} collective-permute-done((bf16[128,2048]{1,0:T(8,128)(2,1)S(1)}, bf16[128,2048]{1,0:T(8,128)(2,1)S(1)}, u32[]{:S(2)}, u32[]{:S(2)}) %collective-permute-start.66) | collective-permute-done | bytes 524320 | tf_op jit(solution)/shard_map/ppermute | solution.py:38
  570.7 6.9 %collective-permute-done.60.refs_1_ = bf16[128,2048]{1,0:T(8,128)(2,1)S(1)} collective-permute-done((bf16[128,2048]{1,0:T(8,128)(2,1)S(1)}, bf16[128,2048]{1,0:T(8,128)(2,1)S(1)}, u32[]{:S(2)}, u32[]{:S(2)}) %collective-permute-start.60) | collective-permute-done | bytes 524320 | tf_op jit(solution)/shard_map/ppermute | solution.py:28
  577.9 3.3 collective-permute-start.68
  583.4 7.6 %collective-permute-done.61.refs_1_ = bf16[128,2048]{1,0:T(8,128)(2,1)S(1)} collective-permute-done((bf16[128,2048]{1,0:T(8,128)(2,1)S(1)}, bf16[128,2048]{1,0:T(8,128)(2,1)S(1)}, u32[]{:S(2)}, u32[]{:S(2)}) %collective-permute-start.61) | collective-permute-done | bytes 524320 | tf_op jit(solution)/shard_map/ppermute | solution.py:28
  591.3 3.3 collective-permute-done.64.refs_1_
  596.9 4.3 collective-permute-done.70.refs_1_
  601.7 3.3 collective-permute-done.71.refs_1_
  605.0 4.5 collective-permute-done.72.refs_1_
  611.6 5.5 collective-permute-done.73.refs_1_
  (188 shorter events, 80.4 us)
Async XLA Ops:
  0.7 18.1 %collective-permute-start = (bf16[128,2048]{1,0:T(8,128)(2,1)}, bf16[128,2048]{1,0:T(8,128)(2,1)S(1)}, u32[]{:S(2)}, u32[]{:S(2)}) collective-permute-start(bf16[128,2048]{1,0:T(8,128)(2,1)} %bitcast.6), channel_id=1, source_target_pairs={{0,2},{1,3},{2,4},{3,5},{4,6},{5,7},{6,8},{7,9},{8,10},{9,11},{10,... | collective-permute-start | bytes 1572872 | tf_op jit(solution)/shard_map/ppermute | solution.py:28
  2.6 16.1 %collective-permute-start.1 = (bf16[128,2048]{1,0:T(8,128)(2,1)}, bf16[128,2048]{1,0:T(8,128)(2,1)S(1)}, u32[]{:S(2)}, u32[]{:S(2)}) collective-permute-start(bf16[128,2048]{1,0:T(8,128)(2,1)} %bitcast.7), channel_id=1, source_target_pairs={{0,14},{1,15},{2,0},{3,1},{4,2},{5,3},{6,4},{7,5},{8,6},{9,7},{10,... | collective-permute-start | bytes 1572872 | tf_op jit(solution)/shard_map/ppermute | solution.py:33
  18.7 14.3 %collective-permute-start.3 = (bf16[128,2048]{1,0:T(8,128)(2,1)S(1)}, bf16[128,2048]{1,0:T(8,128)(2,1)S(1)}, u32[]{:S(2)}, u32[]{:S(2)}) collective-permute-start(bf16[128,2048]{1,0:T(8,128)(2,1)S(1)} %collective-permute-done.refs_1_), channel_id=1, source_target_pairs={{0,2},{1,3},{2,4},{3,5},{4,6},{5,7},{6,8},{7,9},{8,10},{9,11},{10,... | collective-permute-start | bytes 1572872 | tf_op jit(solution)/shard_map/ppermute | solution.py:28
  18.7 34.8 %collective-permute-start.4 = (bf16[128,2048]{1,0:T(8,128)(2,1)S(1)}, bf16[128,2048]{1,0:T(8,128)(2,1)}, u32[]{:S(2)}, u32[]{:S(2)}) collective-permute-start(bf16[128,2048]{1,0:T(8,128)(2,1)S(1)} %collective-permute-done.1.refs_2_), channel_id=1, source_target_pairs={{0,14},{1,15},{2,0},{3,1},{4,2},{5,3},{6,4},{7,5},{8,6},{9,7},{10,... | collective-permute-start | bytes 1572872 | tf_op jit(solution)/shard_map/ppermute | solution.py:33
  33.0 24.1 %collective-permute-start.6 = (bf16[128,2048]{1,0:T(8,128)(2,1)S(1)}, bf16[128,2048]{1,0:T(8,128)(2,1)}, u32[]{:S(2)}, u32[]{:S(2)}) collective-permute-start(bf16[128,2048]{1,0:T(8,128)(2,1)S(1)} %collective-permute-done.3.refs_4_), channel_id=1, source_target_pairs={{0,2},{1,3},{2,4},{3,5},{4,6},{5,7},{6,8},{7,9},{8,10},{9,11},{10,... | collective-permute-start | bytes 1572872 | tf_op jit(solution)/shard_map/ppermute | solution.py:28
  47.9 8.7 %collective-permute-start.18 = (f32[1,2176]{1,0:T(1,128)S(1)}, f32[1,2176]{1,0:T(1,128)S(1)}, u32[]{:S(2)}, u32[]{:S(2)}) collective-permute-start(f32[1,2176]{1,0:T(1,128)S(1)} %add.33.refs_0_), channel_id=1, source_target_pairs={{0,8},{1,9},{2,10},{3,11},{4,12},{5,13},{6,14},{7,15},{8,0},{9,1},... | collective-permute-start | bytes 26120 | tf_op jit(solution)/shard_map/ppermute | solution.py:43
  51.5 17.2 %collective-permute-start.8 = (bf16[128,2048]{1,0:T(8,128)(2,1)S(1)}, bf16[128,2048]{1,0:T(8,128)(2,1)}, u32[]{:S(2)}, u32[]{:S(2)}) collective-permute-start(bf16[128,2048]{1,0:T(8,128)(2,1)S(1)} %collective-permute-done.1.refs_2_), channel_id=1, source_target_pairs={{0,1},{1,0},{2,3},{3,2},{4,5},{5,4},{6,7},{7,6},{8,9},{9,8},{10,11... | collective-permute-start | bytes 1572872 | tf_op jit(solution)/shard_map/ppermute | solution.py:38
  52.1 25.7 %collective-permute-start.5 = (bf16[128,2048]{1,0:T(8,128)(2,1)S(1)}, bf16[128,2048]{1,0:T(8,128)(2,1)}, u32[]{:S(2)}, u32[]{:S(2)}) collective-permute-start(bf16[128,2048]{1,0:T(8,128)(2,1)S(1)} %collective-permute-done.refs_1_), channel_id=1, source_target_pairs={{0,1},{1,0},{2,3},{3,2},{4,5},{5,4},{6,7},{7,6},{8,9},{9,8},{10,11... | collective-permute-start | bytes 1572872 | tf_op jit(solution)/shard_map/ppermute | solution.py:38
  53.6 26.7 %collective-permute-start.7 = (bf16[128,2048]{1,0:T(8,128)(2,1)}, bf16[128,2048]{1,0:T(8,128)(2,1)}, u32[]{:S(2)}, u32[]{:S(2)}) collective-permute-start(bf16[128,2048]{1,0:T(8,128)(2,1)} %collective-permute-done.4.refs_5_), channel_id=1, source_target_pairs={{0,14},{1,15},{2,0},{3,1},{4,2},{5,3},{6,4},{7,5},{8,6},{9,7},{10,... | collective-permute-start | bytes 1572872 | tf_op jit(solution)/shard_map/ppermute | solution.py:33
  56.6 32.3 %collective-permute-start.2 = (bf16[128,2048]{1,0:T(8,128)(2,1)}, bf16[128,2048]{1,0:T(8,128)(2,1)}, u32[]{:S(2)}, u32[]{:S(2)}) collective-permute-start(bf16[128,2048]{1,0:T(8,128)(2,1)} %bitcast.8), channel_id=1, source_target_pairs={{0,1},{1,0},{2,3},{3,2},{4,5},{5,4},{6,7},{7,6},{8,9},{9,8},{10,11... | collective-permute-start | bytes 1572872 | tf_op jit(solution)/shard_map/ppermute | solution.py:38
  57.2 43.0 %collective-permute-start.11 = (bf16[128,2048]{1,0:T(8,128)(2,1)}, bf16[128,2048]{1,0:T(8,128)(2,1)}, u32[]{:S(2)}, u32[]{:S(2)}) collective-permute-start(bf16[128,2048]{1,0:T(8,128)(2,1)} %collective-permute-done.6.refs_7_), channel_id=1, source_target_pairs={{0,1},{1,0},{2,3},{3,2},{4,5},{5,4},{6,7},{7,6},{8,9},{9,8},{10,11... | collective-permute-start | bytes 1572872 | tf_op jit(solution)/shard_map/ppermute | solution.py:38
  68.7 37.1 %collective-permute-start.10 = (bf16[128,2048]{1,0:T(8,128)(2,1)}, bf16[128,2048]{1,0:T(8,128)(2,1)}, u32[]{:S(2)}, u32[]{:S(2)}) collective-permute-start(bf16[128,2048]{1,0:T(8,128)(2,1)} %collective-permute-done.8.refs_9_), channel_id=1, source_target_pairs={{0,14},{1,15},{2,0},{3,1},{4,2},{5,3},{6,4},{7,5},{8,6},{9,7},{10,... | collective-permute-start | bytes 1572872 | tf_op jit(solution)/shard_map/ppermute | solution.py:33
  77.7 28.1 %collective-permute-start.9 = (bf16[128,2048]{1,0:T(8,128)(2,1)}, bf16[128,2048]{1,0:T(8,128)(2,1)}, u32[]{:S(2)}, u32[]{:S(2)}) collective-permute-start(bf16[128,2048]{1,0:T(8,128)(2,1)} %collective-permute-done.5.refs_6_), channel_id=1, source_target_pairs={{0,2},{1,3},{2,4},{3,5},{4,6},{5,7},{6,8},{7,9},{8,10},{9,11},{10,... | collective-permute-start | bytes 1572872 | tf_op jit(solution)/shard_map/ppermute | solution.py:28
  80.2 26.5 %collective-permute-start.14 = (bf16[128,2048]{1,0:T(8,128)(2,1)}, bf16[128,2048]{1,0:T(8,128)(2,1)}, u32[]{:S(2)}, u32[]{:S(2)}) collective-permute-start(bf16[128,2048]{1,0:T(8,128)(2,1)} %collective-permute-done.7.refs_8_), channel_id=1, source_target_pairs={{0,1},{1,0},{2,3},{3,2},{4,5},{5,4},{6,7},{7,6},{8,9},{9,8},{10,11... | collective-permute-start | bytes 1572872 | tf_op jit(solution)/shard_map/ppermute | solution.py:38
  89.0 17.7 %collective-permute-start.13 = (bf16[128,2048]{1,0:T(8,128)(2,1)}, bf16[128,2048]{1,0:T(8,128)(2,1)}, u32[]{:S(2)}, u32[]{:S(2)}) collective-permute-start(bf16[128,2048]{1,0:T(8,128)(2,1)} %collective-permute-done.7.refs_8_), channel_id=1, source_target_pairs={{0,14},{1,15},{2,0},{3,1},{4,2},{5,3},{6,4},{7,5},{8,6},{9,7},{10,... | collective-permute-start | bytes 1572872 | tf_op jit(solution)/shard_map/ppermute | solution.py:33
  100.2 10.9 %collective-permute-start.12 = (bf16[128,2048]{1,0:T(8,128)(2,1)}, bf16[128,2048]{1,0:T(8,128)(2,1)}, u32[]{:S(2)}, u32[]{:S(2)}) collective-permute-start(bf16[128,2048]{1,0:T(8,128)(2,1)} %collective-permute-done.11.refs_12_), channel_id=1, source_target_pairs={{0,2},{1,3},{2,4},{3,5},{4,6},{5,7},{6,8},{7,9},{8,10},{9,11},{10,... | collective-permute-start | bytes 1572872 | tf_op jit(solution)/shard_map/ppermute | solution.py:28
  127.5 5.2 collective-permute-start.21
  134.5 9.2 %collective-permute-start.22 = (bf16[64,2048]{1,0:T(8,128)(2,1)S(1)}, bf16[64,2048]{1,0:T(8,128)(2,1)S(1)}, u32[]{:S(2)}, u32[]{:S(2)}) collective-permute-start(bf16[64,2048]{1,0:T(8,128)(2,1)S(1)} %get-tuple-element.250), channel_id=1, source_target_pairs={{0,16},{16,32},{32,48},{48,64},{1,17},{17,33},{33,49},{49,65},{2,1... | collective-permute-start | bytes 786440 | tf_op jit(solution)/shard_map/ppermute | solution.py:380
  150.9 54.9 %collective-permute-start.29 = (bf16[64,2048]{1,0:T(8,128)(2,1)S(1)}, bf16[64,2048]{1,0:T(8,128)(2,1)S(1)}, u32[]{:S(2)}, u32[]{:S(2)}) collective-permute-start(bf16[64,2048]{1,0:T(8,128)(2,1)S(1)} %get-tuple-element.292), channel_id=1, source_target_pairs={{112,128},{128,144},{144,160},{160,176},{113,129},{129,145},{145,1... | collective-permute-start | bytes 786440 | tf_op jit(solution)/shard_map/ppermute | solution.py:380
  206.3 19.4 %collective-permute-start.30 = (bf16[64,2048]{1,0:T(8,128)(2,1)S(1)}, bf16[64,2048]{1,0:T(8,128)(2,1)S(1)}, u32[]{:S(2)}, u32[]{:S(2)}) collective-permute-start(bf16[64,2048]{1,0:T(8,128)(2,1)S(1)} %get-tuple-element.298), channel_id=1, source_target_pairs={{128,144},{144,160},{160,176},{176,192},{129,145},{145,161},{161,1... | collective-permute-start | bytes 786440 | tf_op jit(solution)/shard_map/ppermute | solution.py:380
  225.8 19.8 %collective-permute-start.31 = (bf16[64,2048]{1,0:T(8,128)(2,1)S(1)}, bf16[64,2048]{1,0:T(8,128)(2,1)S(1)}, u32[]{:S(2)}, u32[]{:S(2)}) collective-permute-start(bf16[64,2048]{1,0:T(8,128)(2,1)S(1)} %get-tuple-element.304), channel_id=1, source_target_pairs={{144,160},{160,176},{176,192},{192,208},{145,161},{161,177},{177,1... | collective-permute-start | bytes 786440 | tf_op jit(solution)/shard_map/ppermute | solution.py:380
  245.6 19.8 %collective-permute-start.32 = (bf16[64,2048]{1,0:T(8,128)(2,1)S(1)}, bf16[64,2048]{1,0:T(8,128)(2,1)S(1)}, u32[]{:S(2)}, u32[]{:S(2)}) collective-permute-start(bf16[64,2048]{1,0:T(8,128)(2,1)S(1)} %get-tuple-element.310), channel_id=1, source_target_pairs={{160,176},{176,192},{192,208},{208,224},{161,177},{177,193},{193,2... | collective-permute-start | bytes 786440 | tf_op jit(solution)/shard_map/ppermute | solution.py:380
  265.4 19.5 %collective-permute-start.33 = (bf16[64,2048]{1,0:T(8,128)(2,1)S(1)}, bf16[64,2048]{1,0:T(8,128)(2,1)S(1)}, u32[]{:S(2)}, u32[]{:S(2)}) collective-permute-start(bf16[64,2048]{1,0:T(8,128)(2,1)S(1)} %get-tuple-element.316), channel_id=1, source_target_pairs={{176,192},{192,208},{208,224},{224,240},{177,193},{193,209},{209,2... | collective-permute-start | bytes 786440 | tf_op jit(solution)/shard_map/ppermute | solution.py:380
  290.2 67.2 %collective-permute-start.40 = (bf16[64,2048]{1,0:T(8,128)(2,1)S(1)}, bf16[64,2048]{1,0:T(8,128)(2,1)S(1)}, u32[]{:S(2)}, u32[]{:S(2)}) collective-permute-start(bf16[64,2048]{1,0:T(8,128)(2,1)S(1)} %get-tuple-element.355), channel_id=1, source_target_pairs={{192,176},{208,192},{224,208},{240,224},{193,177},{209,193},{225,2... | collective-permute-start | bytes 786440 | tf_op jit(solution)/shard_map/ppermute | solution.py:391
  357.5 20.5 %collective-permute-start.41 = (bf16[64,2048]{1,0:T(8,128)(2,1)S(1)}, bf16[64,2048]{1,0:T(8,128)(2,1)S(1)}, u32[]{:S(2)}, u32[]{:S(2)}) collective-permute-start(bf16[64,2048]{1,0:T(8,128)(2,1)S(1)} %get-tuple-element.358), channel_id=1, source_target_pairs={{176,160},{192,176},{208,192},{224,208},{177,161},{193,177},{209,1... | collective-permute-start | bytes 786440 | tf_op jit(solution)/shard_map/ppermute | solution.py:391
  378.5 20.5 %collective-permute-start.42 = (bf16[64,2048]{1,0:T(8,128)(2,1)S(1)}, bf16[64,2048]{1,0:T(8,128)(2,1)S(1)}, u32[]{:S(2)}, u32[]{:S(2)}) collective-permute-start(bf16[64,2048]{1,0:T(8,128)(2,1)S(1)} %get-tuple-element.361), channel_id=1, source_target_pairs={{160,144},{176,160},{192,176},{208,192},{161,145},{177,161},{193,1... | collective-permute-start | bytes 786440 | tf_op jit(solution)/shard_map/ppermute | solution.py:391
  399.0 20.5 %collective-permute-start.43 = (bf16[64,2048]{1,0:T(8,128)(2,1)S(1)}, bf16[64,2048]{1,0:T(8,128)(2,1)S(1)}, u32[]{:S(2)}, u32[]{:S(2)}) collective-permute-start(bf16[64,2048]{1,0:T(8,128)(2,1)S(1)} %get-tuple-element.364), channel_id=1, source_target_pairs={{144,128},{160,144},{176,160},{192,176},{145,129},{161,145},{177,1... | collective-permute-start | bytes 786440 | tf_op jit(solution)/shard_map/ppermute | solution.py:391
  419.6 20.5 %collective-permute-start.44 = (bf16[64,2048]{1,0:T(8,128)(2,1)S(1)}, bf16[64,2048]{1,0:T(8,128)(2,1)S(1)}, u32[]{:S(2)}, u32[]{:S(2)}) collective-permute-start(bf16[64,2048]{1,0:T(8,128)(2,1)S(1)} %get-tuple-element.367), channel_id=1, source_target_pairs={{128,112},{144,128},{160,144},{176,160},{129,113},{145,129},{161,1... | collective-permute-start | bytes 786440 | tf_op jit(solution)/shard_map/ppermute | solution.py:391
  444.7 52.4 %collective-permute-start.51 = (bf16[64,2048]{1,0:T(8,128)(2,1)S(1)}, bf16[64,2048]{1,0:T(8,128)(2,1)S(1)}, u32[]{:S(2)}, u32[]{:S(2)}) collective-permute-start(bf16[64,2048]{1,0:T(8,128)(2,1)S(1)} %get-tuple-element.388), channel_id=1, source_target_pairs={{16,0},{32,16},{48,32},{64,48},{17,1},{33,17},{49,33},{65,49},{18,... | collective-permute-start | bytes 786440 | tf_op jit(solution)/shard_map/ppermute | solution.py:391
  498.9 10.1 %collective-permute-start.52 = (bf16[64,2048]{1,0:T(8,128)(2,1)S(1)}, bf16[64,2048]{1,0:T(8,128)(2,1)S(1)}, u32[]{:S(2)}, u32[]{:S(2)}) collective-permute-start(bf16[64,2048]{1,0:T(8,128)(2,1)S(1)} %get-tuple-element.391), channel_id=1, source_target_pairs={{16,0},{32,16},{48,32},{17,1},{33,17},{49,33},{18,2},{34,18},{50,3... | collective-permute-start | bytes 786440 | tf_op jit(solution)/shard_map/ppermute | solution.py:391
  510.9 10.1 %collective-permute-start.53 = (bf16[64,2048]{1,0:T(8,128)(2,1)S(1)}, bf16[64,2048]{1,0:T(8,128)(2,1)S(1)}, u32[]{:S(2)}, u32[]{:S(2)}) collective-permute-start(bf16[64,2048]{1,0:T(8,128)(2,1)S(1)} %get-tuple-element.394), channel_id=1, source_target_pairs={{16,0},{32,16},{17,1},{33,17},{18,2},{34,18},{19,3},{35,19},{20,4}... | collective-permute-start | bytes 786440 | tf_op jit(solution)/shard_map/ppermute | solution.py:391
  522.9 8.6 %collective-permute-start.54 = (bf16[64,2048]{1,0:T(8,128)(2,1)S(1)}, bf16[64,2048]{1,0:T(8,128)(2,1)S(1)}, u32[]{:S(2)}, u32[]{:S(2)}) collective-permute-start(bf16[64,2048]{1,0:T(8,128)(2,1)S(1)} %get-tuple-element.397), channel_id=1, source_target_pairs={{16,0},{17,1},{18,2},{19,3},{20,4},{21,5},{22,6},{23,7},{24,8},{25... | collective-permute-start | bytes 786440 | tf_op jit(solution)/shard_map/ppermute | solution.py:391
  536.5 14.9 %collective-permute-start.65 = (bf16[128,2048]{1,0:T(8,128)(2,1)S(1)}, bf16[128,2048]{1,0:T(8,128)(2,1)S(1)}, u32[]{:S(2)}, u32[]{:S(2)}) collective-permute-start(bf16[128,2048]{1,0:T(8,128)(2,1)S(1)} %get-tuple-element.416), channel_id=1, source_target_pairs={{0,14},{1,15},{2,0},{3,1},{4,2},{5,3},{6,4},{7,5},{8,6},{9,7},{10,... | collective-permute-start | bytes 1572872 | tf_op jit(solution)/shard_map/ppermute | solution.py:33
  541.8 14.2 %collective-permute-start.58 = (bf16[128,2048]{1,0:T(8,128)(2,1)S(1)}, bf16[128,2048]{1,0:T(8,128)(2,1)S(1)}, u32[]{:S(2)}, u32[]{:S(2)}) collective-permute-start(bf16[128,2048]{1,0:T(8,128)(2,1)S(1)} %get-tuple-element.408), channel_id=1, source_target_pairs={{0,1},{1,0},{2,3},{3,2},{4,5},{5,4},{6,7},{7,6},{8,9},{9,8},{10,11... | collective-permute-start | bytes 1572872 | tf_op jit(solution)/shard_map/ppermute | solution.py:38
  542.0 14.5 %collective-permute-start.59 = (bf16[128,2048]{1,0:T(8,128)(2,1)S(1)}, bf16[128,2048]{1,0:T(8,128)(2,1)S(1)}, u32[]{:S(2)}, u32[]{:S(2)}) collective-permute-start(bf16[128,2048]{1,0:T(8,128)(2,1)S(1)} %get-tuple-element.409), channel_id=1, source_target_pairs={{0,2},{1,3},{2,4},{3,5},{4,6},{5,7},{6,8},{7,9},{8,10},{9,11},{10,... | collective-permute-start | bytes 1572872 | tf_op jit(solution)/shard_map/ppermute | solution.py:28
  551.5 13.5 %collective-permute-start.66 = (bf16[128,2048]{1,0:T(8,128)(2,1)S(1)}, bf16[128,2048]{1,0:T(8,128)(2,1)S(1)}, u32[]{:S(2)}, u32[]{:S(2)}) collective-permute-start(bf16[128,2048]{1,0:T(8,128)(2,1)S(1)} %add.41), channel_id=1, source_target_pairs={{0,1},{1,0},{2,3},{3,2},{4,5},{5,4},{6,7},{7,6},{8,9},{9,8},{10,11... | collective-permute-start | bytes 1572872 | tf_op jit(solution)/shard_map/ppermute | solution.py:38
  551.6 16.6 %collective-permute-start.56 = (bf16[128,2048]{1,0:T(8,128)(2,1)S(1)}, bf16[128,2048]{1,0:T(8,128)(2,1)S(1)}, u32[]{:S(2)}, u32[]{:S(2)}) collective-permute-start(bf16[128,2048]{1,0:T(8,128)(2,1)S(1)} %get-tuple-element.405), channel_id=1, source_target_pairs={{0,2},{1,3},{2,4},{3,5},{4,6},{5,7},{6,8},{7,9},{8,10},{9,11},{10,... | collective-permute-start | bytes 1572872 | tf_op jit(solution)/shard_map/ppermute | solution.py:28
  552.2 18.1 %collective-permute-start.63 = (bf16[128,2048]{1,0:T(8,128)(2,1)S(1)}, bf16[128,2048]{1,0:T(8,128)(2,1)S(1)}, u32[]{:S(2)}, u32[]{:S(2)}) collective-permute-start(bf16[128,2048]{1,0:T(8,128)(2,1)S(1)} %get-tuple-element.412), channel_id=1, source_target_pairs={{0,14},{1,15},{2,0},{3,1},{4,2},{5,3},{6,4},{7,5},{8,6},{9,7},{10,... | collective-permute-start | bytes 1572872 | tf_op jit(solution)/shard_map/ppermute | solution.py:33
  556.7 20.8 %collective-permute-start.60 = (bf16[128,2048]{1,0:T(8,128)(2,1)S(1)}, bf16[128,2048]{1,0:T(8,128)(2,1)S(1)}, u32[]{:S(2)}, u32[]{:S(2)}) collective-permute-start(bf16[128,2048]{1,0:T(8,128)(2,1)S(1)} %add.37), channel_id=1, source_target_pairs={{0,2},{1,3},{2,4},{3,5},{4,6},{5,7},{6,8},{7,9},{8,10},{9,11},{10,... | collective-permute-start | bytes 1572872 | tf_op jit(solution)/shard_map/ppermute | solution.py:28
  565.2 12.6 %collective-permute-start.67 = (bf16[128,2048]{1,0:T(8,128)(2,1)S(1)}, bf16[128,2048]{1,0:T(8,128)(2,1)S(1)}, u32[]{:S(2)}, u32[]{:S(2)}) collective-permute-start(bf16[128,2048]{1,0:T(8,128)(2,1)S(1)} %add.42), channel_id=1, source_target_pairs={{0,14},{1,15},{2,0},{3,1},{4,2},{5,3},{6,4},{7,5},{8,6},{9,7},{10,... | collective-permute-start | bytes 1572872 | tf_op jit(solution)/shard_map/ppermute | solution.py:33
  568.4 14.9 %collective-permute-start.57 = (bf16[128,2048]{1,0:T(8,128)(2,1)S(1)}, bf16[128,2048]{1,0:T(8,128)(2,1)S(1)}, u32[]{:S(2)}, u32[]{:S(2)}) collective-permute-start(bf16[128,2048]{1,0:T(8,128)(2,1)S(1)} %add.35), channel_id=1, source_target_pairs={{0,1},{1,0},{2,3},{3,2},{4,5},{5,4},{6,7},{7,6},{8,9},{9,8},{10,11... | collective-permute-start | bytes 1572872 | tf_op jit(solution)/shard_map/ppermute | solution.py:38
  570.5 24.0 %collective-permute-start.64 = (bf16[128,2048]{1,0:T(8,128)(2,1)S(1)}, bf16[128,2048]{1,0:T(8,128)(2,1)S(1)}, u32[]{:S(2)}, u32[]{:S(2)}) collective-permute-start(bf16[128,2048]{1,0:T(8,128)(2,1)S(1)} %add.40), channel_id=1, source_target_pairs={{0,1},{1,0},{2,3},{3,2},{4,5},{5,4},{6,7},{7,6},{8,9},{9,8},{10,11... | collective-permute-start | bytes 1572872 | tf_op jit(solution)/shard_map/ppermute | solution.py:38
  577.7 13.3 %collective-permute-start.61 = (bf16[128,2048]{1,0:T(8,128)(2,1)S(1)}, bf16[128,2048]{1,0:T(8,128)(2,1)S(1)}, u32[]{:S(2)}, u32[]{:S(2)}) collective-permute-start(bf16[128,2048]{1,0:T(8,128)(2,1)S(1)} %add.38), channel_id=1, source_target_pairs={{0,2},{1,3},{2,4},{3,5},{4,6},{5,7},{6,8},{7,9},{8,10},{9,11},{10,... | collective-permute-start | bytes 1572872 | tf_op jit(solution)/shard_map/ppermute | solution.py:28
  577.9 16.6 %collective-permute-start.68 = (bf16[128,2048]{1,0:T(8,128)(2,1)S(1)}, bf16[128,2048]{1,0:T(8,128)(2,1)S(1)}, u32[]{:S(2)}, u32[]{:S(2)}) collective-permute-start(bf16[128,2048]{1,0:T(8,128)(2,1)S(1)} %add.43), channel_id=1, source_target_pairs={{0,14},{1,15},{2,0},{3,1},{4,2},{5,3},{6,4},{7,5},{8,6},{9,7},{10,... | collective-permute-start | bytes 1572872 | tf_op jit(solution)/shard_map/ppermute | solution.py:33
  581.2 36.4 %collective-permute-start.55 = (bf16[128,2048]{1,0:T(8,128)(2,1)S(1)}, bf16[128,2048]{1,0:T(8,128)(2,1)S(1)}, u32[]{:S(2)}, u32[]{:S(2)}) collective-permute-start(bf16[128,2048]{1,0:T(8,128)(2,1)S(1)} %get-tuple-element.402), channel_id=1, source_target_pairs={{0,1},{1,0},{2,3},{3,2},{4,5},{5,4},{6,7},{7,6},{8,9},{9,8},{10,11... | collective-permute-start | bytes 1572872 | tf_op jit(solution)/shard_map/ppermute | solution.py:38
  591.2 26.5 %collective-permute-start.62 = (bf16[128,2048]{1,0:T(8,128)(2,1)S(1)}, bf16[128,2048]{1,0:T(8,128)(2,1)S(1)}, u32[]{:S(2)}, u32[]{:S(2)}) collective-permute-start(bf16[128,2048]{1,0:T(8,128)(2,1)S(1)} %add.39), channel_id=1, source_target_pairs={{0,2},{1,3},{2,4},{3,5},{4,6},{5,7},{6,8},{7,9},{8,10},{9,11},{10,... | collective-permute-start | bytes 1572872 | tf_op jit(solution)/shard_map/ppermute | solution.py:28
  594.8 22.9 %collective-permute-start.69 = (bf16[128,2048]{1,0:T(8,128)(2,1)S(1)}, bf16[128,2048]{1,0:T(8,128)(2,1)S(1)}, u32[]{:S(2)}, u32[]{:S(2)}) collective-permute-start(bf16[128,2048]{1,0:T(8,128)(2,1)S(1)} %add.44), channel_id=1, source_target_pairs={{0,14},{1,15},{2,0},{3,1},{4,2},{5,3},{6,4},{7,5},{8,6},{9,7},{10,... | collective-permute-start | bytes 1572872 | tf_op jit(solution)/shard_map/ppermute | solution.py:33
  609.5 7.6 %collective-permute-start.73 = (f32[1,2048]{1,0:T(1,128)S(1)}, f32[1,2048]{1,0:T(1,128)S(1)}, u32[]{:S(2)}, u32[]{:S(2)}) collective-permute-start(f32[1,2048]{1,0:T(1,128)S(1)} %add.49.refs_0_), channel_id=1, source_target_pairs={{0,8},{1,9},{2,10},{3,11},{4,12},{5,13},{6,14},{7,15},{8,0},{9,1},... | collective-permute-start | bytes 24584 | tf_op jit(solution)/shard_map/ppermute | solution.py:43
  (32 other events, 428.6 us)

commit v2 on v1

--- a/solution.py
+++ b/solution.py
@@ -41,6 +41,21 @@
 def from_partner(value, distance):
     n = lax.axis_size("fsdp")
     return lax.ppermute(value, "fsdp", [(i, i ^ distance) for i in range(n)])
+
+
+def crossed(section, sections):
+    return (section // 2) % 2 if section < sections - 1 else 0
+
+
+def hop(value, first, last, step):
+    sections, n = lax.axis_size("section"), lax.axis_size("fsdp")
+    route = []
+    for s in range(max(first, 0), min(last, sections - 1) + 1):
+        t = s + step
+        if 0 <= t < sections:
+            flip = crossed(s, sections) ^ crossed(t, sections)
+            route += [(s * n + f, t * n + (f ^ flip)) for f in range(n)]
+    return lax.ppermute(value, ("section", "fsdp"), route) if route else value
 
 
 GATHER = (
@@ -293,6 +308,82 @@
     )(*pieces, fresh, top)
 
 
+def small_kernel(seq_count, gains, new, old, ids, out):
+    me = lax.axis_index("fsdp")
+    share = gains.shape[1]
+    micro_batches = new.shape[0]
+    out[...] = jnp.zeros_like(out)
+    row = lax.broadcasted_iota(jnp.int32, (out.shape[0], share), 0)
+    wide = jnp.where(row == me // 2, gains[...].astype(f32), 0.0)
+    out[:, :share] = jnp.where(me % 2 == 0, wide, 0.0)
+    out[:, share : 2 * share] = jnp.where(me % 2 == 1, wide, 0.0)
+    drift = new[...] - old[...]
+    lane = lax.broadcasted_iota(jnp.int32, (micro_batches, 128), 1)
+    sums = jnp.zeros((micro_batches, 128), f32)
+    counts = jnp.zeros((micro_batches, 128), f32)
+    for k in range(seq_count):
+        member = ids[...] == k
+        total = jnp.sum(jnp.where(member, drift, 0.0), axis=1, keepdims=True)
+        number = jnp.sum(jnp.where(member, 1.0, 0.0), axis=1, keepdims=True)
+        sums = jnp.where(lane == k, total, sums)
+        counts = jnp.where(lane == k, number, counts)
+    out[:micro_batches, 2 * share :] = sums
+    out[micro_batches : 2 * micro_batches, 2 * share :] = counts
+
+
+def small_part(gains, new, old, ids, seq_count, shards):
+    share = gains.shape[1]
+    return pl.pallas_call(
+        functools.partial(small_kernel, seq_count),
+        in_specs=[vmem()] * 4,
+        out_specs=vmem(),
+        out_shape=jax.ShapeDtypeStruct((shards // 2, 2 * share + 128), f32),
+        compiler_params=params(8),
+        name="small_part",
+    )(gains, new, old, ids)
+
+
+def coef_kernel(small, advantages, ids, direction, gain, loss, top):
+    micro_batches, seq_count = advantages.shape
+    pair = small.shape[1] - 128
+    for r in range(small.shape[0]):
+        gain[:, r * pair : (r + 1) * pair] = small[r : r + 1, :pair]
+    sums = small[:micro_batches, pair : pair + seq_count]
+    counts = small[micro_batches : 2 * micro_batches, pair : pair + seq_count]
+    adv = advantages[...]
+    ratio = jnp.exp(sums / counts)
+    bounded = jnp.clip(ratio, 1.0 - clip_epsilon, 1.0 + clip_epsilon) * adv
+    plain = ratio * adv
+    least = jnp.sum(jnp.minimum(plain, bounded), axis=1, keepdims=True)
+    loss[...] = -jnp.sum(least, axis=0, keepdims=True)
+    per_seq = jnp.where(plain <= bounded, -adv * ratio / counts, 0.0)
+    labels = ids[...]
+    coef = jnp.zeros(labels.shape, f32)
+    for k in range(seq_count):
+        coef = coef + jnp.where(labels == k, per_seq[:, k : k + 1], 0.0)
+    n = labels.shape[1]
+    same = lax.broadcasted_iota(jnp.int32, (n, n), 0) == lax.broadcasted_iota(jnp.int32, (n, n), 1)
+    for m in range(micro_batches):
+        column = jnp.sum(jnp.where(same, coef[m : m + 1], 0.0), axis=1, keepdims=True)
+        top[m] = (column * direction[m].astype(f32)).astype(bf16)
+
+
+def coefficients(small, advantages, ids, direction):
+    width = direction.shape[-1]
+    return pl.pallas_call(
+        coef_kernel,
+        in_specs=[vmem()] * 4,
+        out_specs=[vmem()] * 3,
+        out_shape=[
+            jax.ShapeDtypeStruct((1, width), f32),
+            jax.ShapeDtypeStruct((1, 1), f32),
+            jax.ShapeDtypeStruct(direction.shape, bf16),
+        ],
+        compiler_params=params(8),
+        name="coefficients",
+    )(small, advantages, ids, direction)
+
+
 def add_kernel(*refs):
     out = refs[-1]
     acc = refs[0][...].astype(f32)
@@ -331,64 +422,41 @@
     rows = row_count // SPLIT
     share = width // shards
 
-    labels = lax.broadcasted_iota(jnp.int32, (1, 1, seq_count), 2)
-    member = (segment_ids[:, :, None] == labels).astype(f32)
-    log_drift = new_logprob - old_logprob
-    part_sums = jnp.sum(log_drift[:, :, None] * member, axis=1)
-    part_counts = jnp.sum(member, axis=1)
-    spread = jnp.zeros((1, width), f32)
-    spread = lax.dynamic_update_slice(spread, section_gains.astype(f32), (0, shard * share))
-    table = micro_batches * seq_count
-    small = jnp.concatenate(
-        [spread, part_sums.reshape(1, table), part_counts.reshape(1, table),
-         jnp.zeros((1, 128 - 2 * table), f32)], axis=1
-    )
+    small = small_part(section_gains, new_logprob, old_logprob, segment_ids, seq_count, shards)
 
     held = {(0, 0): section_weights[0]}
     distance = 1
-    for i, (sent, move, got) in enumerate(GATHER):
-        held[got] = MOVE[move](held[sent])
-        if i % 3 == 2 and distance < shards:
+    for step in range(0, len(GATHER), 3):
+        came = [MOVE[move](held[sent]) for sent, move, _ in GATHER[step : step + 3]]
+        if distance < shards:
             small = add(small, from_partner(small, distance))
             distance *= 2
-
-    gain = small[:, :width]
-    seq_sums = small[:, width : width + table].reshape(micro_batches, seq_count)
-    seq_counts = small[:, width + table : width + 2 * table].reshape(micro_batches, seq_count)
-    seq_ratio = jnp.exp(seq_sums / seq_counts)
-    clipped = jnp.clip(seq_ratio, 1.0 - clip_epsilon, 1.0 + clip_epsilon)
-    plain_term = seq_ratio * advantages
-    bounded_term = clipped * advantages
-    gspo_loss = -jnp.sum(jnp.minimum(plain_term, bounded_term))
-    per_seq = jnp.where(plain_term <= bounded_term, -advantages * seq_ratio / seq_counts, 0.0)
-    token_coef = jnp.sum(member * per_seq[:, None, :], axis=2)
-    top_grad = (token_coef[:, :, None] * top_direction.astype(f32)).astype(bf16)
+        came, small = lax.optimization_barrier((came, small))
+        held.update(zip([entry[2] for entry in GATHER[step : step + 3]], came))
+
+    gain, gspo_loss, top_grad = coefficients(small, advantages, segment_ids, top_direction)
     top_grad = top_grad.reshape(count, rows, width)
     fresh = embeddings.reshape(count, rows, width)
     pieces = [held[key] for key in KEYS]
-    pieces, fresh, top_grad, gain, gspo_loss = lax.optimization_barrier(
-        (pieces, fresh, top_grad, gain, gspo_loss)
-    )
+    pieces, fresh, top_grad, gain = lax.optimization_barrier((pieces, fresh, top_grad, gain))
     matrix, fresh, top_grad = assemble(pieces, fresh, top_grad)
 
     ticks = count + sections - 1
     state, kept = None, None
     for tick in range(ticks):
         state, kept = forward_tick(tick, count, fresh, state, matrix, gain, kept)
-        route = [(s, s + 1) for s in range(sections - 1) if 0 <= tick - s < count]
-        if route:
-            state = lax.ppermute(state, "section", route)
+        even = tick - tick % 2
+        if tick < ticks - 1:
+            state = hop(state, even + 1 - count, even + 1, 1)
 
     state, grads = None, None
     for tick in range(ticks):
         state, grads = backward_tick(
             tick, count, sections, top_grad, state, kept[4], gain, kept, grads
         )
-        route = [
-            (s, s - 1) for s in range(1, sections) if 0 <= tick - (sections - 1 - s) < count
-        ]
-        if route:
-            state = lax.ppermute(state, "section", route)
+        even = tick - tick % 2
+        if tick < ticks - 1:
+            state = hop(state, sections - 2 - even, sections - 2 - even + count, -1)
 
     tokens = count * rows
     partials = weight_partials(
@@ -405,10 +473,11 @@
         if distance < shards:
             gain_total = add(gain_total, from_partner(gain_total, distance), kind=f32)
             distance *= 2
+        came, gain_total = lax.optimization_barrier((came, gain_total))
         for home, values in came.items():
             total[home] = add(total[home], *values, kind=f32 if home == (0, 0) else bf16)
     gain_share = lax.dynamic_slice(gain_total, (0, shard * share), (1, share))
-    return (total[0, 0][None], gain_share, gspo_loss)
+    return (total[0, 0][None], gain_share, gspo_loss[0, 0])
 
 
 def solution(mesh):

time: 630 us -> 479 us (0.76)
  the two profiles are of different devices: /device:TPU:2 before, /device:TPU:1 now
where the time goes in v2:
time: 479 us; the launch traced here: 470 us
  waiting for transfers between devices  306 us (64%)
  starting transfers between devices  121 us (25%)
  Pallas kernels  34 us (7%)
  local copies, waits for them, and re-layouts  7.38 us (2%)
    ppermute x36, waiting for transfers between devices, hop(): return lax.ppermute(value, ('section', 'fsdp'), route) if route else value  218 us
    ppermute x36, starting transfers between devices, hop(): return lax.ppermute(value, ('section', 'fsdp'), route) if route else value  71.2 us
    ppermute x8, waiting for transfers between devices, from_partner(): return lax.ppermute(value, 'fsdp', [(i, i ^ distance) for i in range(n)])  54.4 us
    ppermute x10, starting transfers between devices, from_z_above(): return lax.ppermute(value, 'fsdp', [(i, (i - 2) % n) for i in range(n)])  20.6 us
    pallas_call x19, Pallas kernels, backward_tick(): pl.pallas_call(functools.partial(backward_kernel, tick, count, sections,...  15.8 us
    ppermute x10, waiting for transfers between devices, from_z_above(): return lax.ppermute(value, 'fsdp', [(i, (i - 2) % n) for i in range(n)])  13.8 us
    ppermute x10, waiting for transfers between devices, from_z_below(): return lax.ppermute(value, 'fsdp', [(i, (i + 2) % n) for i in range(n)])  11.7 us
    pallas_call x19, Pallas kernels, forward_tick(): pl.pallas_call(functools.partial(forward_kernel, tick, count, first), in_...  11.3 us
  transfers between devices with their start and end apart: 74, of which 34 were waited for; matrix products, arithmetic and copies ran while one was open for 0% of the time, Pallas kernels for 0%

profile of v2, /device:TPU:1, one launch (start us, length us, event | category | flops | bytes accessed | tf_op | source)
XLA Modules:
  0.0 470.0 jit_solution(15796053439803502413)
XLA Ops:
  0.6 2.5 collective-permute-start
  3.2 4.0 collective-permute-start.1
  11.5 8.7 %collective-permute-done.3.refs_1_ = f32[8,384]{1,0:T(8,128)S(1)} collective-permute-done((f32[8,384]{1,0:T(8,128)S(1)}, f32[8,384]{1,0:T(8,128)S(1)}, u32[]{:S(2)}, u32[]{:S(2)}) %collective-permute-start.3) | collective-permute-done | bytes 12320 | tf_op jit(solution)/shard_map/ppermute | solution.py:43
  20.3 2.7 collective-permute-start.5
  24.4 7.8 %collective-permute-done.7.refs_1_ = f32[8,384]{1,0:T(8,128)S(1)} collective-permute-done((f32[8,384]{1,0:T(8,128)S(1)}, f32[8,384]{1,0:T(8,128)S(1)}, u32[]{:S(2)}, u32[]{:S(2)}) %collective-permute-start.7) | collective-permute-done | bytes 12320 | tf_op jit(solution)/shard_map/ppermute | solution.py:43
  33.9 2.7 collective-permute-start.9
  38.1 5.3 %collective-permute-done.11.refs_1_ = f32[8,384]{1,0:T(8,128)S(1)} collective-permute-done((f32[8,384]{1,0:T(8,128)S(1)}, f32[8,384]{1,0:T(8,128)S(1)}, u32[]{:S(2)}, u32[]{:S(2)}) %collective-permute-start.11) | collective-permute-done | bytes 12320 | tf_op jit(solution)/shard_map/ppermute | solution.py:43
  47.1 3.3 collective-permute-start.15
  50.4 3.8 collective-permute-done.15.refs_1_
  55.5 4.6 collective-permute-start.16
  60.2 4.4 collective-permute-done.17.refs_14_
  64.6 3.6 collective-permute-done.16.refs_13_
  74.5 16.7 %collective-permute-start.19 = (bf16[64,2048]{1,0:T(8,128)(2,1)S(1)}, bf16[64,2048]{1,0:T(8,128)(2,1)S(1)}, u32[]{:S(2)}, u32[]{:S(2)}) collective-permute-start(bf16[64,2048]{1,0:T(8,128)(2,1)S(1)} %get-tuple-element.296), channel_id=1, source_target_pairs={{0,16},{1,17},{2,18},{3,19},{4,20},{5,21},{6,22},{7,23},{8,24},{9,... | collective-permute-start | bytes 786440 | tf_op jit(solution)/shard_map/ppermute | solution.py:58
  91.2 3.3 collective-permute-done.19.refs_1_
  96.3 4.2 collective-permute-start.20
  100.5 3.3 collective-permute-done.20.refs_1_
  105.6 5.6 %collective-permute-start.21 = (bf16[64,2048]{1,0:T(8,128)(2,1)S(1)}, bf16[64,2048]{1,0:T(8,128)(2,1)S(1)}, u32[]{:S(2)}, u32[]{:S(2)}) collective-permute-start(bf16[64,2048]{1,0:T(8,128)(2,1)S(1)} %get-tuple-element.308), channel_id=1, source_target_pairs={{0,16},{1,17},{2,18},{3,19},{4,20},{5,21},{6,22},{7,23},{8,24},{9,... | collective-permute-start | bytes 786440 | tf_op jit(solution)/shard_map/ppermute | solution.py:58
  111.2 3.3 collective-permute-done.21.refs_1_
  116.2 5.6 %collective-permute-start.22 = (bf16[64,2048]{1,0:T(8,128)(2,1)S(1)}, bf16[64,2048]{1,0:T(8,128)(2,1)S(1)}, u32[]{:S(2)}, u32[]{:S(2)}) collective-permute-start(bf16[64,2048]{1,0:T(8,128)(2,1)S(1)} %get-tuple-element.314), channel_id=1, source_target_pairs={{0,16},{1,17},{2,18},{3,19},{4,20},{5,21},{6,22},{7,23},{8,24},{9,... | collective-permute-start | bytes 786440 | tf_op jit(solution)/shard_map/ppermute | solution.py:58
  121.8 3.3 collective-permute-done.22.refs_0_
  125.1 2.1 forward_layer_4.1
  127.3 5.6 %collective-permute-start.23 = (bf16[64,2048]{1,0:T(8,128)(2,1)S(1)}, bf16[64,2048]{1,0:T(8,128)(2,1)S(1)}, u32[]{:S(2)}, u32[]{:S(2)}) collective-permute-start(bf16[64,2048]{1,0:T(8,128)(2,1)S(1)} %get-tuple-element.320), channel_id=1, source_target_pairs={{16,33},{17,32},{18,35},{19,34},{20,37},{21,36},{22,39},{23,38},{2... | collective-permute-start | bytes 786440 | tf_op jit(solution)/shard_map/ppermute | solution.py:58
  132.9 3.3 collective-permute-done.23.refs_0_
  136.5 7.0 %collective-permute-start.24 = (bf16[64,2048]{1,0:T(8,128)(2,1)S(1)}, bf16[64,2048]{1,0:T(8,128)(2,1)S(1)}, u32[]{:S(2)}, u32[]{:S(2)}) collective-permute-start(bf16[64,2048]{1,0:T(8,128)(2,1)S(1)} %get-tuple-element.326), channel_id=1, source_target_pairs={{16,33},{17,32},{18,35},{19,34},{20,37},{21,36},{22,39},{23,38},{2... | collective-permute-start | bytes 786440 | tf_op jit(solution)/shard_map/ppermute | solution.py:58
  143.6 3.3 collective-permute-done.24.refs_0_
  158.5 2.2 backward_layer_0.1
  164.3 5.0 %backward_layer_5.1 = (bf16[64,2048]{1,0:T(8,128)(2,1)S(1)}, bf16[4,64,2048]{2,1,0:T(8,128)(2,1)S(1)}, f32[1,2048]{1,0:T(1,128)S(1)}) custom-call(bf16[64,2048]{1,0:T(8,128)(2,1)S(1)} %collective-permute-done.41.refs_0_, bf16[2048,2048]{1,0:T(8,128)(2,1)S(1)} %get-tuple-element.406.refs_1_.refs_2_, ...), custom_call_target="tpu_custom_call", output_to_operand_aliasing={{1}: (6, {}), {2}: (7, {})} | custom-call | tf_op jit(solution)/shard_map/backward_layer_5/pallas_call | solution.py:237
  175.7 8.3 %collective-permute-done.49.refs_0_ = bf16[64,2048]{1,0:T(8,128)(2,1)S(1)} collective-permute-done((bf16[64,2048]{1,0:T(8,128)(2,1)S(1)}, bf16[64,2048]{1,0:T(8,128)(2,1)S(1)}, u32[]{:S(2)}, u32[]{:S(2)}) %collective-permute-start.49) | collective-permute-done | bytes 262176 | tf_op jit(solution)/shard_map/ppermute | solution.py:58
  185.5 160.2 %collective-permute-done.50.refs_0_ = bf16[64,2048]{1,0:T(8,128)(2,1)S(1)} collective-permute-done((bf16[64,2048]{1,0:T(8,128)(2,1)S(1)}, bf16[64,2048]{1,0:T(8,128)(2,1)S(1)}, u32[]{:S(2)}, u32[]{:S(2)}) %collective-permute-start.50) | collective-permute-done | bytes 262176 | tf_op jit(solution)/shard_map/ppermute | solution.py:58
  349.5 7.9 %collective-permute-done.51.refs_0_ = bf16[64,2048]{1,0:T(8,128)(2,1)S(1)} collective-permute-done((bf16[64,2048]{1,0:T(8,128)(2,1)S(1)}, bf16[64,2048]{1,0:T(8,128)(2,1)S(1)}, u32[]{:S(2)}, u32[]{:S(2)}) %collective-permute-start.51) | collective-permute-done | bytes 262176 | tf_op jit(solution)/shard_map/ppermute | solution.py:58
  361.2 7.9 %collective-permute-done.52.refs_0_ = bf16[64,2048]{1,0:T(8,128)(2,1)S(1)} collective-permute-done((bf16[64,2048]{1,0:T(8,128)(2,1)S(1)}, bf16[64,2048]{1,0:T(8,128)(2,1)S(1)}, u32[]{:S(2)}, u32[]{:S(2)}) %collective-permute-start.52) | collective-permute-done | bytes 262176 | tf_op jit(solution)/shard_map/ppermute | solution.py:58
  372.9 7.2 %collective-permute-done.53.refs_0_ = bf16[64,2048]{1,0:T(8,128)(2,1)S(1)} collective-permute-done((bf16[64,2048]{1,0:T(8,128)(2,1)S(1)}, bf16[64,2048]{1,0:T(8,128)(2,1)S(1)}, u32[]{:S(2)}, u32[]{:S(2)}) %collective-permute-start.53) | collective-permute-done | bytes 262176 | tf_op jit(solution)/shard_map/ppermute | solution.py:58
  383.9 7.0 %collective-permute-done.54.refs_0_ = bf16[64,2048]{1,0:T(8,128)(2,1)S(1)} collective-permute-done((bf16[64,2048]{1,0:T(8,128)(2,1)S(1)}, bf16[64,2048]{1,0:T(8,128)(2,1)S(1)}, u32[]{:S(2)}, u32[]{:S(2)}) %collective-permute-start.54) | collective-permute-done | bytes 262176 | tf_op jit(solution)/shard_map/ppermute | solution.py:58
  391.6 2.4 weight_partials.1
  397.7 2.7 collective-permute-start.61
  400.3 7.0 %collective-permute-done.59.refs_1_ = bf16[1,2048]{1,0:T(2,128)(2,1)S(1)} collective-permute-done((bf16[1,2048]{1,0:T(2,128)(2,1)S(1)}, bf16[1,2048]{1,0:T(2,128)(2,1)S(1)}, u32[]{:S(2)}, u32[]{:S(2)}) %collective-permute-start.59) | collective-permute-done | bytes 4128 | tf_op jit(solution)/shard_map/ppermute | solution.py:43
  408.3 3.4 collective-permute-start.60
  413.5 5.9 %collective-permute-done.63.refs_1_ = f32[1,2048]{1,0:T(1,128)S(1)} collective-permute-done((f32[1,2048]{1,0:T(1,128)S(1)}, f32[1,2048]{1,0:T(1,128)S(1)}, u32[]{:S(2)}, u32[]{:S(2)}) %collective-permute-start.63) | collective-permute-done | bytes 8224 | tf_op jit(solution)/shard_map/ppermute | solution.py:43
  419.4 3.2 collective-permute-done.62.refs_1_
  424.9 9.1 %collective-permute-done.67.refs_1_ = f32[1,2048]{1,0:T(1,128)S(1)} collective-permute-done((f32[1,2048]{1,0:T(1,128)S(1)}, f32[1,2048]{1,0:T(1,128)S(1)}, u32[]{:S(2)}, u32[]{:S(2)}) %collective-permute-start.67) | collective-permute-done | bytes 8224 | tf_op jit(solution)/shard_map/ppermute | solution.py:43
  434.0 2.8 collective-permute-done.65.refs_1_
  437.2 2.7 collective-permute-start.69
  439.9 2.7 collective-permute-start.71
  442.9 6.8 %collective-permute-done.71.refs_1_ = f32[1,2048]{1,0:T(1,128)S(1)} collective-permute-done((f32[1,2048]{1,0:T(1,128)S(1)}, f32[1,2048]{1,0:T(1,128)S(1)}, u32[]{:S(2)}, u32[]{:S(2)}) %collective-permute-start.71) | collective-permute-done | bytes 8224 | tf_op jit(solution)/shard_map/ppermute | solution.py:43
  450.3 3.2 collective-permute-start.73
  453.8 2.1 collective-permute-done.55.refs_1_
  455.8 8.5 %collective-permute-done.73.refs_3_ = bf16[128,2048]{1,0:T(8,128)(2,1)S(1)} collective-permute-done((bf16[128,2048]{1,0:T(8,128)(2,1)S(1)}, bf16[128,2048]{1,0:T(8,128)(2,1)S(1)}, u32[]{:S(2)}, u32[]{:S(2)}) %collective-permute-start.73) | collective-permute-done | bytes 524320 | tf_op jit(solution)/shard_map/ppermute | solution.py:33
  464.3 3.6 collective-permute-done.72.refs_2_
  (179 shorter events, 76.0 us)
Async XLA Ops:
  0.6 19.5 %collective-permute-start = (bf16[128,2048]{1,0:T(8,128)(2,1)}, bf16[128,2048]{1,0:T(8,128)(2,1)S(1)}, u32[]{:S(2)}, u32[]{:S(2)}) collective-permute-start(bf16[128,2048]{1,0:T(8,128)(2,1)} %bitcast.7), channel_id=1, source_target_pairs={{0,2},{1,3},{2,4},{3,5},{4,6},{5,7},{6,8},{7,9},{8,10},{9,11},{10,... | collective-permute-start | bytes 1572872 | tf_op jit(solution)/shard_map/ppermute | solution.py:28
  3.2 17.0 %collective-permute-start.1 = (bf16[128,2048]{1,0:T(8,128)(2,1)}, bf16[128,2048]{1,0:T(8,128)(2,1)S(1)}, u32[]{:S(2)}, u32[]{:S(2)}) collective-permute-start(bf16[128,2048]{1,0:T(8,128)(2,1)} %bitcast.8), channel_id=1, source_target_pairs={{0,14},{1,15},{2,0},{3,1},{4,2},{5,3},{6,4},{7,5},{8,6},{9,7},{10,... | collective-permute-start | bytes 1572872 | tf_op jit(solution)/shard_map/ppermute | solution.py:33
  7.2 13.0 %collective-permute-start.2 = (bf16[128,2048]{1,0:T(8,128)(2,1)}, bf16[128,2048]{1,0:T(8,128)(2,1)S(1)}, u32[]{:S(2)}, u32[]{:S(2)}) collective-permute-start(bf16[128,2048]{1,0:T(8,128)(2,1)} %bitcast.9), channel_id=1, source_target_pairs={{0,1},{1,0},{2,3},{3,2},{4,5},{5,4},{6,7},{7,6},{8,9},{9,8},{10,11... | collective-permute-start | bytes 1572872 | tf_op jit(solution)/shard_map/ppermute | solution.py:38
  11.2 9.0 %collective-permute-start.3 = (f32[8,384]{1,0:T(8,128)S(1)}, f32[8,384]{1,0:T(8,128)S(1)}, u32[]{:S(2)}, u32[]{:S(2)}) collective-permute-start(f32[8,384]{1,0:T(8,128)S(1)} %small_part.1.refs_0_), channel_id=1, source_target_pairs={{0,1},{1,0},{2,3},{3,2},{4,5},{5,4},{6,7},{7,6},{8,9},{9,8},{10,11... | collective-permute-start | bytes 36872 | tf_op jit(solution)/shard_map/ppermute | solution.py:43
  20.2 12.8 %collective-permute-start.4 = (bf16[128,2048]{1,0:T(8,128)(2,1)S(1)}, bf16[128,2048]{1,0:T(8,128)(2,1)S(1)}, u32[]{:S(2)}, u32[]{:S(2)}) collective-permute-start(bf16[128,2048]{1,0:T(8,128)(2,1)S(1)} %collective-permute-done.refs_1_), channel_id=1, source_target_pairs={{0,2},{1,3},{2,4},{3,5},{4,6},{5,7},{6,8},{7,9},{8,10},{9,11},{10,... | collective-permute-start | bytes 1572872 | tf_op jit(solution)/shard_map/ppermute | solution.py:28
  20.3 12.8 %collective-permute-start.5 = (bf16[128,2048]{1,0:T(8,128)(2,1)S(1)}, bf16[128,2048]{1,0:T(8,128)(2,1)S(1)}, u32[]{:S(2)}, u32[]{:S(2)}) collective-permute-start(bf16[128,2048]{1,0:T(8,128)(2,1)S(1)} %collective-permute-done.1.refs_2_), channel_id=1, source_target_pairs={{0,14},{1,15},{2,0},{3,1},{4,2},{5,3},{6,4},{7,5},{8,6},{9,7},{10,... | collective-permute-start | bytes 1572872 | tf_op jit(solution)/shard_map/ppermute | solution.py:33
  22.9 11.0 %collective-permute-start.6 = (bf16[128,2048]{1,0:T(8,128)(2,1)S(1)}, bf16[128,2048]{1,0:T(8,128)(2,1)S(1)}, u32[]{:S(2)}, u32[]{:S(2)}) collective-permute-start(bf16[128,2048]{1,0:T(8,128)(2,1)S(1)} %collective-permute-done.refs_1_), channel_id=1, source_target_pairs={{0,1},{1,0},{2,3},{3,2},{4,5},{5,4},{6,7},{7,6},{8,9},{9,8},{10,11... | collective-permute-start | bytes 1572872 | tf_op jit(solution)/shard_map/ppermute | solution.py:38
  24.1 8.0 %collective-permute-start.7 = (f32[8,384]{1,0:T(8,128)S(1)}, f32[8,384]{1,0:T(8,128)S(1)}, u32[]{:S(2)}, u32[]{:S(2)}) collective-permute-start(f32[8,384]{1,0:T(8,128)S(1)} %add.24.refs_0_), channel_id=1, source_target_pairs={{0,2},{1,3},{2,0},{3,1},{4,6},{5,7},{6,4},{7,5},{8,10},{9,11},{10,... | collective-permute-start | bytes 36872 | tf_op jit(solution)/shard_map/ppermute | solution.py:43
  24.1 21.0 %collective-permute-start.10 = (bf16[128,2048]{1,0:T(8,128)(2,1)S(1)}, bf16[128,2048]{1,0:T(8,128)(2,1)S(1)}, u32[]{:S(2)}, u32[]{:S(2)}) collective-permute-start(bf16[128,2048]{1,0:T(8,128)(2,1)S(1)} %collective-permute-done.1.refs_2_), channel_id=1, source_target_pairs={{0,1},{1,0},{2,3},{3,2},{4,5},{5,4},{6,7},{7,6},{8,9},{9,8},{10,11... | collective-permute-start | bytes 1572872 | tf_op jit(solution)/shard_map/ppermute | solution.py:38
  33.9 11.2 %collective-permute-start.8 = (bf16[128,2048]{1,0:T(8,128)(2,1)S(1)}, bf16[128,2048]{1,0:T(8,128)(2,1)S(1)}, u32[]{:S(2)}, u32[]{:S(2)}) collective-permute-start(bf16[128,2048]{1,0:T(8,128)(2,1)S(1)} %collective-permute-done.4.refs_4_), channel_id=1, source_target_pairs={{0,2},{1,3},{2,4},{3,5},{4,6},{5,7},{6,8},{7,9},{8,10},{9,11},{10,... | collective-permute-start | bytes 1572872 | tf_op jit(solution)/shard_map/ppermute | solution.py:28
  33.9 11.2 %collective-permute-start.9 = (bf16[128,2048]{1,0:T(8,128)(2,1)S(1)}, bf16[128,2048]{1,0:T(8,128)(2,1)S(1)}, u32[]{:S(2)}, u32[]{:S(2)}) collective-permute-start(bf16[128,2048]{1,0:T(8,128)(2,1)S(1)} %collective-permute-done.5.refs_5_), channel_id=1, source_target_pairs={{0,14},{1,15},{2,0},{3,1},{4,2},{5,3},{6,4},{7,5},{8,6},{9,7},{10,... | collective-permute-start | bytes 1572872 | tf_op jit(solution)/shard_map/ppermute | solution.py:33
  36.6 18.8 %collective-permute-start.12 = (bf16[128,2048]{1,0:T(8,128)(2,1)S(1)}, bf16[128,2048]{1,0:T(8,128)(2,1)S(1)}, u32[]{:S(2)}, u32[]{:S(2)}) collective-permute-start(bf16[128,2048]{1,0:T(8,128)(2,1)S(1)} %collective-permute-done.6.refs_6_), channel_id=1, source_target_pairs={{0,2},{1,3},{2,4},{3,5},{4,6},{5,7},{6,8},{7,9},{8,10},{9,11},{10,... | collective-permute-start | bytes 1572872 | tf_op jit(solution)/shard_map/ppermute | solution.py:28
  45.2 10.3 %collective-permute-start.13 = (bf16[128,2048]{1,0:T(8,128)(2,1)S(1)}, bf16[128,2048]{1,0:T(8,128)(2,1)S(1)}, u32[]{:S(2)}, u32[]{:S(2)}) collective-permute-start(bf16[128,2048]{1,0:T(8,128)(2,1)S(1)} %collective-permute-done.10.refs_9_), channel_id=1, source_target_pairs={{0,14},{1,15},{2,0},{3,1},{4,2},{5,3},{6,4},{7,5},{8,6},{9,7},{10,... | collective-permute-start | bytes 1572872 | tf_op jit(solution)/shard_map/ppermute | solution.py:33
  45.8 9.7 %collective-permute-start.14 = (bf16[128,2048]{1,0:T(8,128)(2,1)S(1)}, bf16[128,2048]{1,0:T(8,128)(2,1)S(1)}, u32[]{:S(2)}, u32[]{:S(2)}) collective-permute-start(bf16[128,2048]{1,0:T(8,128)(2,1)S(1)} %collective-permute-done.8.refs_7_), channel_id=1, source_target_pairs={{0,1},{1,0},{2,3},{3,2},{4,5},{5,4},{6,7},{7,6},{8,9},{9,8},{10,11... | collective-permute-start | bytes 1572872 | tf_op jit(solution)/shard_map/ppermute | solution.py:38
  50.4 14.2 %collective-permute-start.17 = (bf16[128,2048]{1,0:T(8,128)(2,1)S(1)}, bf16[128,2048]{1,0:T(8,128)(2,1)S(1)}, u32[]{:S(2)}, u32[]{:S(2)}) collective-permute-start(bf16[128,2048]{1,0:T(8,128)(2,1)S(1)} %collective-permute-done.9.refs_8_), channel_id=1, source_target_pairs={{0,14},{1,15},{2,0},{3,1},{4,2},{5,3},{6,4},{7,5},{8,6},{9,7},{10,... | collective-permute-start | bytes 1572872 | tf_op jit(solution)/shard_map/ppermute | solution.py:33
  54.2 10.4 %collective-permute-start.18 = (bf16[128,2048]{1,0:T(8,128)(2,1)S(1)}, bf16[128,2048]{1,0:T(8,128)(2,1)S(1)}, u32[]{:S(2)}, u32[]{:S(2)}) collective-permute-start(bf16[128,2048]{1,0:T(8,128)(2,1)S(1)} %collective-permute-done.9.refs_8_), channel_id=1, source_target_pairs={{0,1},{1,0},{2,3},{3,2},{4,5},{5,4},{6,7},{7,6},{8,9},{9,8},{10,11... | collective-permute-start | bytes 1572872 | tf_op jit(solution)/shard_map/ppermute | solution.py:38
  55.5 12.7 %collective-permute-start.16 = (bf16[128,2048]{1,0:T(8,128)(2,1)S(1)}, bf16[128,2048]{1,0:T(8,128)(2,1)S(1)}, u32[]{:S(2)}, u32[]{:S(2)}) collective-permute-start(bf16[128,2048]{1,0:T(8,128)(2,1)S(1)} %collective-permute-done.14.refs_12_), channel_id=1, source_target_pairs={{0,2},{1,3},{2,4},{3,5},{4,6},{5,7},{6,8},{7,9},{8,10},{9,11},{10,... | collective-permute-start | bytes 1572872 | tf_op jit(solution)/shard_map/ppermute | solution.py:28
  74.5 20.0 %collective-permute-start.19 = (bf16[64,2048]{1,0:T(8,128)(2,1)S(1)}, bf16[64,2048]{1,0:T(8,128)(2,1)S(1)}, u32[]{:S(2)}, u32[]{:S(2)}) collective-permute-start(bf16[64,2048]{1,0:T(8,128)(2,1)S(1)} %get-tuple-element.296), channel_id=1, source_target_pairs={{0,16},{1,17},{2,18},{3,19},{4,20},{5,21},{6,22},{7,23},{8,24},{9,... | collective-permute-start | bytes 786440 | tf_op jit(solution)/shard_map/ppermute | solution.py:58
  96.3 7.5 %collective-permute-start.20 = (bf16[64,2048]{1,0:T(8,128)(2,1)S(1)}, bf16[64,2048]{1,0:T(8,128)(2,1)S(1)}, u32[]{:S(2)}, u32[]{:S(2)}) collective-permute-start(bf16[64,2048]{1,0:T(8,128)(2,1)S(1)} %get-tuple-element.302), channel_id=1, source_target_pairs={{0,16},{1,17},{2,18},{3,19},{4,20},{5,21},{6,22},{7,23},{8,24},{9,... | collective-permute-start | bytes 786440 | tf_op jit(solution)/shard_map/ppermute | solution.py:58
  105.6 8.9 %collective-permute-start.21 = (bf16[64,2048]{1,0:T(8,128)(2,1)S(1)}, bf16[64,2048]{1,0:T(8,128)(2,1)S(1)}, u32[]{:S(2)}, u32[]{:S(2)}) collective-permute-start(bf16[64,2048]{1,0:T(8,128)(2,1)S(1)} %get-tuple-element.308), channel_id=1, source_target_pairs={{0,16},{1,17},{2,18},{3,19},{4,20},{5,21},{6,22},{7,23},{8,24},{9,... | collective-permute-start | bytes 786440 | tf_op jit(solution)/shard_map/ppermute | solution.py:58
  116.2 8.9 %collective-permute-start.22 = (bf16[64,2048]{1,0:T(8,128)(2,1)S(1)}, bf16[64,2048]{1,0:T(8,128)(2,1)S(1)}, u32[]{:S(2)}, u32[]{:S(2)}) collective-permute-start(bf16[64,2048]{1,0:T(8,128)(2,1)S(1)} %get-tuple-element.314), channel_id=1, source_target_pairs={{0,16},{1,17},{2,18},{3,19},{4,20},{5,21},{6,22},{7,23},{8,24},{9,... | collective-permute-start | bytes 786440 | tf_op jit(solution)/shard_map/ppermute | solution.py:58
  127.3 8.9 %collective-permute-start.23 = (bf16[64,2048]{1,0:T(8,128)(2,1)S(1)}, bf16[64,2048]{1,0:T(8,128)(2,1)S(1)}, u32[]{:S(2)}, u32[]{:S(2)}) collective-permute-start(bf16[64,2048]{1,0:T(8,128)(2,1)S(1)} %get-tuple-element.320), channel_id=1, source_target_pairs={{16,33},{17,32},{18,35},{19,34},{20,37},{21,36},{22,39},{23,38},{2... | collective-permute-start | bytes 786440 | tf_op jit(solution)/shard_map/ppermute | solution.py:58
  136.5 10.3 %collective-permute-start.24 = (bf16[64,2048]{1,0:T(8,128)(2,1)S(1)}, bf16[64,2048]{1,0:T(8,128)(2,1)S(1)}, u32[]{:S(2)}, u32[]{:S(2)}) collective-permute-start(bf16[64,2048]{1,0:T(8,128)(2,1)S(1)} %get-tuple-element.326), channel_id=1, source_target_pairs={{16,33},{17,32},{18,35},{19,34},{20,37},{21,36},{22,39},{23,38},{2... | collective-permute-start | bytes 786440 | tf_op jit(solution)/shard_map/ppermute | solution.py:58
  174.4 9.6 %collective-permute-start.49 = (bf16[64,2048]{1,0:T(8,128)(2,1)S(1)}, bf16[64,2048]{1,0:T(8,128)(2,1)S(1)}, u32[]{:S(2)}, u32[]{:S(2)}) collective-permute-start(bf16[64,2048]{1,0:T(8,128)(2,1)S(1)} %get-tuple-element.446), channel_id=1, source_target_pairs={{32,17},{33,16},{34,19},{35,18},{36,21},{37,20},{38,23},{39,22},{4... | collective-permute-start | bytes 786440 | tf_op jit(solution)/shard_map/ppermute | solution.py:58
  184.2 161.5 %collective-permute-start.50 = (bf16[64,2048]{1,0:T(8,128)(2,1)S(1)}, bf16[64,2048]{1,0:T(8,128)(2,1)S(1)}, u32[]{:S(2)}, u32[]{:S(2)}) collective-permute-start(bf16[64,2048]{1,0:T(8,128)(2,1)S(1)} %get-tuple-element.449), channel_id=1, source_target_pairs={{32,17},{33,16},{34,19},{35,18},{36,21},{37,20},{38,23},{39,22},{4... | collective-permute-start | bytes 786440 | tf_op jit(solution)/shard_map/ppermute | solution.py:58
  347.6 9.8 %collective-permute-start.51 = (bf16[64,2048]{1,0:T(8,128)(2,1)S(1)}, bf16[64,2048]{1,0:T(8,128)(2,1)S(1)}, u32[]{:S(2)}, u32[]{:S(2)}) collective-permute-start(bf16[64,2048]{1,0:T(8,128)(2,1)S(1)} %get-tuple-element.452), channel_id=1, source_target_pairs={{16,0},{17,1},{18,2},{19,3},{20,4},{21,5},{22,6},{23,7},{24,8},{25... | collective-permute-start | bytes 786440 | tf_op jit(solution)/shard_map/ppermute | solution.py:58
  359.3 9.8 %collective-permute-start.52 = (bf16[64,2048]{1,0:T(8,128)(2,1)S(1)}, bf16[64,2048]{1,0:T(8,128)(2,1)S(1)}, u32[]{:S(2)}, u32[]{:S(2)}) collective-permute-start(bf16[64,2048]{1,0:T(8,128)(2,1)S(1)} %get-tuple-element.455), channel_id=1, source_target_pairs={{16,0},{17,1},{18,2},{19,3},{20,4},{21,5},{22,6},{23,7},{24,8},{25... | collective-permute-start | bytes 786440 | tf_op jit(solution)/shard_map/ppermute | solution.py:58
  371.0 9.2 %collective-permute-start.53 = (bf16[64,2048]{1,0:T(8,128)(2,1)S(1)}, bf16[64,2048]{1,0:T(8,128)(2,1)S(1)}, u32[]{:S(2)}, u32[]{:S(2)}) collective-permute-start(bf16[64,2048]{1,0:T(8,128)(2,1)S(1)} %get-tuple-element.458), channel_id=1, source_target_pairs={{16,0},{17,1},{18,2},{19,3},{20,4},{21,5},{22,6},{23,7},{24,8},{25... | collective-permute-start | bytes 786440 | tf_op jit(solution)/shard_map/ppermute | solution.py:58
  382.0 8.9 %collective-permute-start.54 = (bf16[64,2048]{1,0:T(8,128)(2,1)S(1)}, bf16[64,2048]{1,0:T(8,128)(2,1)S(1)}, u32[]{:S(2)}, u32[]{:S(2)}) collective-permute-start(bf16[64,2048]{1,0:T(8,128)(2,1)S(1)} %get-tuple-element.461), channel_id=1, source_target_pairs={{16,0},{17,1},{18,2},{19,3},{20,4},{21,5},{22,6},{23,7},{24,8},{25... | collective-permute-start | bytes 786440 | tf_op jit(solution)/shard_map/ppermute | solution.py:58
  394.1 14.1 %collective-permute-start.56 = (bf16[128,2048]{1,0:T(8,128)(2,1)S(1)}, bf16[128,2048]{1,0:T(8,128)(2,1)S(1)}, u32[]{:S(2)}, u32[]{:S(2)}) collective-permute-start(bf16[128,2048]{1,0:T(8,128)(2,1)S(1)} %get-tuple-element.470), channel_id=1, source_target_pairs={{0,14},{1,15},{2,0},{3,1},{4,2},{5,3},{6,4},{7,5},{8,6},{9,7},{10,... | collective-permute-start | bytes 1572872 | tf_op jit(solution)/shard_map/ppermute | solution.py:33
  395.9 12.3 %collective-permute-start.57 = (bf16[128,2048]{1,0:T(8,128)(2,1)S(1)}, bf16[128,2048]{1,0:T(8,128)(2,1)S(1)}, u32[]{:S(2)}, u32[]{:S(2)}) collective-permute-start(bf16[128,2048]{1,0:T(8,128)(2,1)S(1)} %get-tuple-element.471), channel_id=1, source_target_pairs={{0,1},{1,0},{2,3},{3,2},{4,5},{5,4},{6,7},{7,6},{8,9},{9,8},{10,11... | collective-permute-start | bytes 1572872 | tf_op jit(solution)/shard_map/ppermute | solution.py:38
  396.1 12.1 %collective-permute-start.58 = (bf16[128,2048]{1,0:T(8,128)(2,1)S(1)}, bf16[128,2048]{1,0:T(8,128)(2,1)S(1)}, u32[]{:S(2)}, u32[]{:S(2)}) collective-permute-start(bf16[128,2048]{1,0:T(8,128)(2,1)S(1)} %get-tuple-element.472), channel_id=1, source_target_pairs={{0,2},{1,3},{2,4},{3,5},{4,6},{5,7},{6,8},{7,9},{8,10},{9,11},{10,... | collective-permute-start | bytes 1572872 | tf_op jit(solution)/shard_map/ppermute | solution.py:28
  396.2 11.2 %collective-permute-start.59 = (bf16[1,2048]{1,0:T(2,128)(2,1)S(1)}, bf16[1,2048]{1,0:T(2,128)(2,1)S(1)}, u32[]{:S(2)}, u32[]{:S(2)}) collective-permute-start(bf16[1,2048]{1,0:T(2,128)(2,1)S(1)} %add.28.refs_0_), channel_id=1, source_target_pairs={{0,1},{1,0},{2,3},{3,2},{4,5},{5,4},{6,7},{7,6},{8,9},{9,8},{10,11... | collective-permute-start | bytes 12296 | tf_op jit(solution)/shard_map/ppermute | solution.py:43
  397.7 21.7 %collective-permute-start.61 = (bf16[128,2048]{1,0:T(8,128)(2,1)S(1)}, bf16[128,2048]{1,0:T(8,128)(2,1)S(1)}, u32[]{:S(2)}, u32[]{:S(2)}) collective-permute-start(bf16[128,2048]{1,0:T(8,128)(2,1)S(1)} %get-tuple-element.475), channel_id=1, source_target_pairs={{0,14},{1,15},{2,0},{3,1},{4,2},{5,3},{6,4},{7,5},{8,6},{9,7},{10,... | collective-permute-start | bytes 1572872 | tf_op jit(solution)/shard_map/ppermute | solution.py:33
  407.4 15.2 %collective-permute-start.62 = (bf16[128,2048]{1,0:T(8,128)(2,1)S(1)}, bf16[128,2048]{1,0:T(8,128)(2,1)S(1)}, u32[]{:S(2)}, u32[]{:S(2)}) collective-permute-start(bf16[128,2048]{1,0:T(8,128)(2,1)S(1)} %get-tuple-element.476), channel_id=1, source_target_pairs={{0,2},{1,3},{2,4},{3,5},{4,6},{5,7},{6,8},{7,9},{8,10},{9,11},{10,... | collective-permute-start | bytes 1572872 | tf_op jit(solution)/shard_map/ppermute | solution.py:28
  408.3 14.3 %collective-permute-start.60 = (bf16[128,2048]{1,0:T(8,128)(2,1)S(1)}, bf16[128,2048]{1,0:T(8,128)(2,1)S(1)}, u32[]{:S(2)}, u32[]{:S(2)}) collective-permute-start(bf16[128,2048]{1,0:T(8,128)(2,1)S(1)} %add.30), channel_id=1, source_target_pairs={{0,1},{1,0},{2,3},{3,2},{4,5},{5,4},{6,7},{7,6},{8,9},{9,8},{10,11... | collective-permute-start | bytes 1572872 | tf_op jit(solution)/shard_map/ppermute | solution.py:38
  411.8 7.6 %collective-permute-start.63 = (f32[1,2048]{1,0:T(1,128)S(1)}, f32[1,2048]{1,0:T(1,128)S(1)}, u32[]{:S(2)}, u32[]{:S(2)}) collective-permute-start(f32[1,2048]{1,0:T(1,128)S(1)} %add.29.refs_0_), channel_id=1, source_target_pairs={{0,2},{1,3},{2,0},{3,1},{4,6},{5,7},{6,4},{7,5},{8,10},{9,11},{10,... | collective-permute-start | bytes 24584 | tf_op jit(solution)/shard_map/ppermute | solution.py:43
  412.0 22.1 %collective-permute-start.66 = (bf16[128,2048]{1,0:T(8,128)(2,1)S(1)}, bf16[128,2048]{1,0:T(8,128)(2,1)S(1)}, u32[]{:S(2)}, u32[]{:S(2)}) collective-permute-start(bf16[128,2048]{1,0:T(8,128)(2,1)S(1)} %add.34), channel_id=1, source_target_pairs={{0,2},{1,3},{2,4},{3,5},{4,6},{5,7},{6,8},{7,9},{8,10},{9,11},{10,... | collective-permute-start | bytes 1572872 | tf_op jit(solution)/shard_map/ppermute | solution.py:28
  422.7 14.1 %collective-permute-start.65 = (bf16[128,2048]{1,0:T(8,128)(2,1)S(1)}, bf16[128,2048]{1,0:T(8,128)(2,1)S(1)}, u32[]{:S(2)}, u32[]{:S(2)}) collective-permute-start(bf16[128,2048]{1,0:T(8,128)(2,1)S(1)} %add.33), channel_id=1, source_target_pairs={{0,1},{1,0},{2,3},{3,2},{4,5},{5,4},{6,7},{7,6},{8,9},{9,8},{10,11... | collective-permute-start | bytes 1572872 | tf_op jit(solution)/shard_map/ppermute | solution.py:38
  423.1 13.7 %collective-permute-start.64 = (bf16[128,2048]{1,0:T(8,128)(2,1)S(1)}, bf16[128,2048]{1,0:T(8,128)(2,1)S(1)}, u32[]{:S(2)}, u32[]{:S(2)}) collective-permute-start(bf16[128,2048]{1,0:T(8,128)(2,1)S(1)} %add.32), channel_id=1, source_target_pairs={{0,14},{1,15},{2,0},{3,1},{4,2},{5,3},{6,4},{7,5},{8,6},{9,7},{10,... | collective-permute-start | bytes 1572872 | tf_op jit(solution)/shard_map/ppermute | solution.py:33
  423.2 10.8 %collective-permute-start.67 = (f32[1,2048]{1,0:T(1,128)S(1)}, f32[1,2048]{1,0:T(1,128)S(1)}, u32[]{:S(2)}, u32[]{:S(2)}) collective-permute-start(f32[1,2048]{1,0:T(1,128)S(1)} %add.31.refs_0_), channel_id=1, source_target_pairs={{0,4},{1,5},{2,6},{3,7},{4,0},{5,1},{6,2},{7,3},{8,12},{9,13},{10,... | collective-permute-start | bytes 24584 | tf_op jit(solution)/shard_map/ppermute | solution.py:43
  423.4 26.3 %collective-permute-start.68 = (bf16[128,2048]{1,0:T(8,128)(2,1)S(1)}, bf16[128,2048]{1,0:T(8,128)(2,1)S(1)}, u32[]{:S(2)}, u32[]{:S(2)}) collective-permute-start(bf16[128,2048]{1,0:T(8,128)(2,1)S(1)} %add.37), channel_id=1, source_target_pairs={{0,1},{1,0},{2,3},{3,2},{4,5},{5,4},{6,7},{7,6},{8,9},{9,8},{10,11... | collective-permute-start | bytes 1572872 | tf_op jit(solution)/shard_map/ppermute | solution.py:38
  436.9 13.2 %collective-permute-start.70 = (bf16[128,2048]{1,0:T(8,128)(2,1)S(1)}, bf16[128,2048]{1,0:T(8,128)(2,1)S(1)}, u32[]{:S(2)}, u32[]{:S(2)}) collective-permute-start(bf16[128,2048]{1,0:T(8,128)(2,1)S(1)} %add.39), channel_id=1, source_target_pairs={{0,2},{1,3},{2,4},{3,5},{4,6},{5,7},{6,8},{7,9},{8,10},{9,11},{10,... | collective-permute-start | bytes 1572872 | tf_op jit(solution)/shard_map/ppermute | solution.py:28
  437.2 13.0 %collective-permute-start.69 = (bf16[128,2048]{1,0:T(8,128)(2,1)S(1)}, bf16[128,2048]{1,0:T(8,128)(2,1)S(1)}, u32[]{:S(2)}, u32[]{:S(2)}) collective-permute-start(bf16[128,2048]{1,0:T(8,128)(2,1)S(1)} %add.38), channel_id=1, source_target_pairs={{0,14},{1,15},{2,0},{3,1},{4,2},{5,3},{6,4},{7,5},{8,6},{9,7},{10,... | collective-permute-start | bytes 1572872 | tf_op jit(solution)/shard_map/ppermute | solution.py:33
  439.9 9.8 %collective-permute-start.71 = (f32[1,2048]{1,0:T(1,128)S(1)}, f32[1,2048]{1,0:T(1,128)S(1)}, u32[]{:S(2)}, u32[]{:S(2)}) collective-permute-start(f32[1,2048]{1,0:T(1,128)S(1)} %add.35.refs_0_), channel_id=1, source_target_pairs={{0,8},{1,9},{2,10},{3,11},{4,12},{5,13},{6,14},{7,15},{8,0},{9,1},... | collective-permute-start | bytes 24584 | tf_op jit(solution)/shard_map/ppermute | solution.py:43
  442.6 13.2 %collective-permute-start.55 = (bf16[128,2048]{1,0:T(8,128)(2,1)}, bf16[128,2048]{1,0:T(8,128)(2,1)S(1)}, u32[]{:S(2)}, u32[]{:S(2)}) collective-permute-start(bf16[128,2048]{1,0:T(8,128)(2,1)} %get-tuple-element.466), channel_id=1, source_target_pairs={{0,1},{1,0},{2,3},{3,2},{4,5},{5,4},{6,7},{7,6},{8,9},{9,8},{10,11... | collective-permute-start | bytes 1572872 | tf_op jit(solution)/shard_map/ppermute | solution.py:38
  450.3 14.0 %collective-permute-start.73 = (bf16[128,2048]{1,0:T(8,128)(2,1)S(1)}, bf16[128,2048]{1,0:T(8,128)(2,1)S(1)}, u32[]{:S(2)}, u32[]{:S(2)}) collective-permute-start(bf16[128,2048]{1,0:T(8,128)(2,1)S(1)} %add.42), channel_id=1, source_target_pairs={{0,14},{1,15},{2,0},{3,1},{4,2},{5,3},{6,4},{7,5},{8,6},{9,7},{10,... | collective-permute-start | bytes 1572872 | tf_op jit(solution)/shard_map/ppermute | solution.py:33
  453.7 14.3 %collective-permute-start.72 = (bf16[128,2048]{1,0:T(8,128)(2,1)S(1)}, bf16[128,2048]{1,0:T(8,128)(2,1)S(1)}, u32[]{:S(2)}, u32[]{:S(2)}) collective-permute-start(bf16[128,2048]{1,0:T(8,128)(2,1)S(1)} %add.41), channel_id=1, source_target_pairs={{0,2},{1,3},{2,4},{3,5},{4,6},{5,7},{6,8},{7,9},{8,10},{9,11},{10,... | collective-permute-start | bytes 1572872 | tf_op jit(solution)/shard_map/ppermute | solution.py:28
  (34 other events, 37.4 us)
